TPU v7x, 128 devices: a whole 4x4x4 slice. The times are simulated.
128 devices in a mesh: island: 8 (over y, z_lo), fsdp: 16 (over z_hi, x, core).
Axes of the slice: x: 4, y: 4, z: 4 (z_hi: 2, z_lo: 2; z = z_hi * 2 + z_lo), core: 2. Of those that a mesh axis runs over, the one named last changes fastest.
Arguments:
- tokens: bfloat16 [98304, 4096], P(('island', 'fsdp')), may hold values from -3 to 3
- key_cotangent: bfloat16 [98304, 1024], P(('island', 'fsdp')), may hold values from -3 to 3
- local_keys: bfloat16 [8, 4, 4096, 1024], P('island', None, 'fsdp'), may hold values from -0.09375 to 0.09375
- pseudo_codes: int32 [8, 4096, 1024], P('island', 'fsdp'), may hold values from -127 to 127
- code_exponents: int32 [8, 4096, 8], P('island', 'fsdp'), may hold values from -15 to -13
- outer_weights: float32 [4096, 1024], P('fsdp'), may hold values from -0.09375 to 0.09375
- outer_momentum: float32 [4096, 1024], P('fsdp'), may hold values from -0.02 to 0.02
- fragment: int32 [8], P('island'), may hold values from 0 to 3
Outputs:
- input_grads: bfloat16 [98304, 4096], P(('island', 'fsdp'))
- weight_grads: bfloat16 [8, 4096, 1024], P('island', 'fsdp')
- new_weights: float32 [4096, 1024], P('fsdp')
- new_momentum: float32 [4096, 1024], P('fsdp')
- synced_keys: bfloat16 [8, 4096, 1024], P('island', 'fsdp')
Inputs may be any that keep to these rules, and one draw needn't show every extreme that they name: `fragment`: for each island, an index into the block's layers.
All inputs are finite; a program needn't handle non-finite values.
Results may differ from a plain program's by a relative error of at most 0.019.
Values may be sent and summed in bfloat16 or wider, within the bound.
No kernel may reach another device: no remote copies, remote signals or barrier semaphores. Data moves between devices by JAX's collectives and lax.ppermute only.
A program may use at most 128 MiB of HBM per device.

v0:
```python
import jax
import jax.numpy as jnp
from jax import lax
from jax.sharding import PartitionSpec as P

momentum_rate = 0.9
outer_rate = 0.7
keep_share = 0.5


def local(
    tokens,
    key_cotangent,
    local_keys,
    pseudo_codes,
    code_exponents,
    outer_weights,
    outer_momentum,
    fragment,
):
    key_layer = local_keys[0, local_keys.shape[1] - 1]
    row_count = key_layer.shape[0]
    input_grads = jnp.einsum(
        "tk,dk->td",
        key_cotangent,
        lax.all_gather(key_layer, "fsdp", axis=0, tiled=True),
        preferred_element_type=jnp.float32,
    ).astype(jnp.bfloat16)
    weight_grads = lax.psum_scatter(
        jnp.einsum("td,tk->dk", tokens, key_cotangent, preferred_element_type=jnp.float32).astype(
            jnp.bfloat16
        ),
        "fsdp",
        scatter_dimension=0,
        tiled=True,
    )[None]
    scales = jnp.exp2(code_exponents[0].astype(jnp.float32))
    scaled_codes = (
        pseudo_codes[0].reshape(row_count, scales.shape[1], -1).astype(jnp.float32)
        * scales[:, :, None]
    )
    island_delta = scaled_codes.reshape(row_count, -1)
    islands = lax.axis_size("island")
    mean_delta = lax.psum(island_delta.astype(jnp.bfloat16), "island").astype(jnp.float32) / islands
    new_momentum = momentum_rate * outer_momentum + mean_delta
    new_weights = outer_weights - outer_rate * (mean_delta + momentum_rate * new_momentum)
    chosen = lax.dynamic_index_in_dim(local_keys[0], fragment[0], 0, keepdims=False)
    synced_keys = (
        keep_share * chosen.astype(jnp.float32) + (1.0 - keep_share) * new_weights
    ).astype(jnp.bfloat16)[None]
    return (input_grads, weight_grads, new_weights, new_momentum, synced_keys)


def solution(mesh):
    placed = (
        P(("island", "fsdp"), None),
        P(("island", "fsdp"), None),
        P("island", None, "fsdp", None),
        P("island", "fsdp", None),
        P("island", "fsdp", None),
        P("fsdp", None),
        P("fsdp", None),
        P("island"),
    )
    return jax.shard_map(
        local,
        mesh=mesh,
        in_specs=placed,
        out_specs=(
            P(("island", "fsdp"), None),
            P("island", "fsdp", None),
            P("fsdp", None),
            P("fsdp", None),
            P("island", "fsdp", None),
        ),
        check_vma=False,
    )
```

profile of v0, /device:TPU:1, one launch (start us, length us, event | category | flops | bytes accessed | tf_op | source)
XLA Modules:
  0.0 203.1 jit_solution(4857308899498602486)
XLA Ops:
  8.0 0.0 copy-start
  8.0 0.0 all-reduce.2.cloned.1.call-start
  8.1 0.8 exponential_bitcast_fusion
  8.9 0.1 copy.13
  9.0 0.3 mul.27
  9.3 2.3 %fusion.5 = bf16[256,1024]{1,0:T(8,128)(2,1)} fusion(f32[32,8,8,128]{3,2,1,0:T(8,128)S(1)} %bitcast.27, s32[1,256,1024]{2,1,0:T(8,128)} %param.11), kind=kLoop, calls=%fused_computation.5 | loop fusion | flops 786432 | bytes 2621440 | tf_op jit(solution)/shard_map/convert_element_type | solution.py:44
  11.6 0.0 all-reduce.2.cloned.1.call-update
  11.7 0.0 all-gather.3.cloned.1.call-start
  11.7 1.9 slice.3
  13.6 0.0 all-gather.3.cloned.1.call-update
  13.6 0.0 reduce-scatter.2.cloned.1.call-start
  13.7 0.0 copy-done
  13.7 11.8 %convolution_convert_fusion = bf16[4096,1024]{1,0:T(8,128)(2,1)} fusion(bf16[768,4096]{1,0:T(8,128)(2,1)} %param.8, bf16[768,1024]{1,0:T(8,128)(2,1)S(1)} %copy-done), kind=kOutput, calls=%fused_computation.2 | convolution fusion | flops 6446645248 | bytes 16252928 | tf_op jit(solution)/shard_map/td,tk->dk/dot_general | solution.py:30
  25.5 0.0 copy-start.1
  25.5 0.0 reduce-scatter.2.cloned.1.call-update
  26.2 72.7 %all-reduce.2.cloned.1.call-done = bf16[256,1024]{1,0:T(8,128)(2,1)} async-done(((bf16[256,1024]{1,0:T(8,128)(2,1)}), bf16[256,1024]{1,0:T(8,128)(2,1)}) %all-reduce.2.cloned.1.call-update) | async-done | bytes 524304 | tf_op jit(solution)/shard_map/psum | solution.py:44
  98.9 0.0 copy-done.1
  98.9 3.4 %fusion.8 = (bf16[1,256,1024]{2,1,0:T(8,128)(2,1)}, f32[256,1024]{1,0:T(8,128)}, f32[256,1024]{1,0:T(8,128)}) fusion(bf16[1,4,256,1024]{3,2,1,0:T(8,128)(2,1)} %param.10, s32[]{:T(128)S(6)} %select_n.4, f32[256,1024]{1,0:T(8,128)S(1)} %copy-done.1, bf16[256,1024]{1,0:T(8,128)(2,1)} %all-reduce.2.cloned.1.call-done, f32[256,1024]{1,0:T(8,128)} %param.14), kind=kLoop, calls=%fused_computation.12 | loop fusion | flops 3145728 | bytes 5767172 | tf_op jit(solution)/shard_map/broadcast_in_dim | solution.py:48
  102.4 0.0 all-gather.3.cloned.1.call-done
  102.4 12.5 %fusion.2 = bf16[768,4096]{1,0:T(8,128)(2,1)} fusion(bf16[768,1024]{1,0:T(8,128)(2,1)S(1)} %copy-done, bf16[1,1,4096,1024]{3,2,1,0:T(8,128)(2,1)} %all-gather.3.cloned.1.call-done), kind=kOutput, calls=%fused_computation.3 | convolution fusion | flops 6445596672 | bytes 16252928 | tf_op jit(solution)/shard_map/tk,dk->td/dot_general | solution.py:23
  114.9 80.8 %reduce-scatter.2.cloned.1.call-done = bf16[256,1024]{1,0:T(8,128)(2,1)} async-done(((bf16[4096,1024]{1,0:T(8,128)(2,1)}), bf16[256,1024]{1,0:T(8,128)(2,1)}) %reduce-scatter.2.cloned.1.call-update) | async-done | bytes 524304 | tf_op jit(solution)/shard_map/reduce_scatter | solution.py:29
Async XLA Ops:
  8.0 5.7 %copy-start = (bf16[768,1024]{1,0:T(8,128)(2,1)S(1)}, bf16[768,1024]{1,0:T(8,128)(2,1)}, u32[]{:S(2)}) copy-start(bf16[768,1024]{1,0:T(8,128)(2,1)} %param.9) | copy-start | bytes 4718596
  8.0 90.9 %all-reduce.2.cloned.1.call-start = ((), (), s32[]{:S(2)}) async-start(), calls=%async_computation.2 | async-start | bytes 1048576 | tf_op jit(solution)/shard_map/psum | solution.py:44
  11.7 90.7 %all-gather.3.cloned.1.call-start = ((), (), s32[]{:S(2)}) async-start(), calls=%async_computation.3 | async-start | bytes 8912896 | tf_op jit(solution)/shard_map/all_gather | solution.py:26
  13.6 182.1 %reduce-scatter.2.cloned.1.call-start = ((), (), s32[]{:S(2)}) async-start(), calls=%async_computation.1 | async-start | bytes 8912896 | tf_op jit(solution)/shard_map/reduce_scatter | solution.py:29
  25.5 73.5 %copy-start.1 = (f32[256,1024]{1,0:T(8,128)S(1)}, f32[256,1024]{1,0:T(8,128)}, u32[]{:S(2)}) copy-start(f32[256,1024]{1,0:T(8,128)} %param.13) | copy-start | bytes 3145732
Sparse Core Ops, SparseCore 0:
  11.9 86.9 all-reduce.1
Sparse Core Ops, SparseCore 1:
  15.2 77.5 all-gather.2
  97.5 98.1 reduce-scatter.1
where the time goes:
time: 204 us; the launch traced here: 203 us
  waiting for transfers between devices  154 us (75%)
  matrix products  24.3 us (12%)
  between operations  16.2 us (8%)
  other arithmetic  6.54 us (3%)
  local copies, waits for them, and re-layouts  2.35 us (1%)
    reduce_scatter x1, waiting for transfers between devices, local(): lax.psum_scatter(jnp.einsum('td,tk->dk', tokens, key_cotangent, preferred...  80.8 us
    psum x1, waiting for transfers between devices, local(): lax.psum(island_delta.astype(jnp.bfloat16), 'island').astype(jnp.float32)  72.7 us
    dot_general x1, matrix products, local(): jnp.einsum('tk,dk->td', key_cotangent, lax.all_gather(key_layer, 'fsdp',...  12.5 us
    dot_general x1, matrix products, local(): jnp.einsum('td,tk->dk', tokens, key_cotangent, preferred_element_type=jnp...  11.8 us
  transfers between devices with their start and end apart: 3, of which 2 were waited for; matrix products, arithmetic and copies ran while one was open for 15% of the time, Pallas kernels for 0%

commit v1 on v0

v1 whole, which is shorter than its diff:
```python
import jax
import jax.numpy as jnp
from jax import lax
from jax.experimental import pallas as pl
from jax.experimental.pallas import tpu as pltpu
from jax.sharding import PartitionSpec as P

momentum_rate = 0.9
outer_rate = 0.7
keep_share = 0.5

BLK = 256
PR = 144
QR = BLK - PR
MIB = 1 << 20


def fsdp_perm(move):
    pairs = []
    for h in range(2):
        for x in range(4):
            for c in range(2):
                h2, x2, c2 = move(h, x, c)
                pairs.append((h * 8 + x * 2 + c, (h2 % 2) * 8 + (x2 % 4) * 2 + c2))
    return pairs


def block_at(place, dh, dx):
    return (place ^ (dh << 3)) & 9 | ((((place >> 1) + dx) & 3) << 1)


def to_x(value, step):
    return lax.ppermute(value, "fsdp", fsdp_perm(lambda h, x, c: (h, x + step, c)))


def to_z(value):
    return lax.ppermute(value, "fsdp", fsdp_perm(lambda h, x, c: (h + 1, x, c)))


def to_core(value):
    return lax.ppermute(value, "fsdp", fsdp_perm(lambda h, x, c: (h, x, 1 - c)))


def params(mib):
    return pltpu.CompilerParams(vmem_limit_bytes=mib * MIB)


def term(tok, kc):
    return lax.dot_general(tok, kc, (((0,), (0,)), ((), ())), preferred_element_type=jnp.float32)


def partner_terms(order, tokens, kc):
    rows, width = kc.shape

    def body(order_ref, tok_ref, kc_ref, out_ref):
        out_ref[0] = term(tok_ref[...], kc_ref[...]).astype(jnp.bfloat16)

    return pl.pallas_call(
        body,
        grid_spec=pltpu.PrefetchScalarGridSpec(
            num_scalar_prefetch=1,
            grid=(8,),
            in_specs=[
                pl.BlockSpec((rows, BLK), lambda j, order: (0, block_at(order[0], j >> 2, j & 3))),
                pl.BlockSpec((rows, width), lambda j, order: (0, 0)),
            ],
            out_specs=pl.BlockSpec((1, BLK, width), lambda j, order: (j, 0, 0)),
        ),
        out_shape=jax.ShapeDtypeStruct((8, BLK, width), jnp.bfloat16),
        compiler_params=params(32),
        cost_estimate=pl.CostEstimate(
            flops=2 * 8 * rows * BLK * width, bytes_accessed=9 * MIB, transcendentals=0
        ),
        name="partner_terms",
    )(order, tokens, kc)


def own_terms(order, tokens, kc, received):
    rows, width = kc.shape

    def body(order_ref, tok_ref, kc_ref, got_ref, zp, kp, x1, x2, x3, kq):
        j = pl.program_id(0)
        total = term(tok_ref[...], kc_ref[...]) + got_ref[0].astype(jnp.float32)
        total = total.astype(jnp.bfloat16)
        for k in range(8):
            dh, dx = k // 4, k % 4

            @pl.when(j == k)
            def _():
                (zp if dh else kp)[dx] = total[:PR]
                (kq, x1, x2, x3)[dx][dh] = total[PR:]

    def whole(shape):
        return pl.BlockSpec(shape, lambda j, order: (0,) * len(shape))

    shapes = [(4, PR, width)] * 2 + [(2, QR, width)] * 4
    return pl.pallas_call(
        body,
        grid_spec=pltpu.PrefetchScalarGridSpec(
            num_scalar_prefetch=1,
            grid=(8,),
            in_specs=[
                pl.BlockSpec((rows, BLK), lambda j, order: (0, block_at(order[0], j >> 2, j & 3))),
                whole((rows, width)),
                pl.BlockSpec((1, BLK, width), lambda j, order: (j, 0, 0)),
            ],
            out_specs=[whole(s) for s in shapes],
        ),
        out_shape=[jax.ShapeDtypeStruct(s, jnp.bfloat16) for s in shapes],
        compiler_params=params(40),
        cost_estimate=pl.CostEstimate(
            flops=2 * 8 * rows * BLK * width, bytes_accessed=13 * MIB, transcendentals=0
        ),
        name="own_terms",
    )(order, tokens, kc, received)


def input_part(order, side, kc, blocks, out):
    rows, width = kc.shape
    stacked = len(blocks) == 1

    def body(order_ref, kc_ref, *rest):
        refs, out_ref = rest[: len(blocks)], rest[-1]
        j = pl.program_id(0)

        def product(block):
            out_ref[...] = lax.dot_general(
                kc_ref[...], block, (((1,), (1,)), ((), ())), preferred_element_type=jnp.float32
            ).astype(jnp.bfloat16)

        if stacked:
            product(refs[0][0])
        else:
            for k in range(4):

                @pl.when(j == k)
                def _():
                    product(refs[k][...])

    def whole(shape):
        return pl.BlockSpec(shape, lambda j, order: (0,) * len(shape))

    if stacked:
        block_specs = [pl.BlockSpec((1, BLK, width), lambda j, order: (j, 0, 0))]
    else:
        block_specs = [whole((BLK, width))] * 4
    operands = [order, kc, *blocks]
    in_specs = [whole((rows, width)), *block_specs]
    aliases = {}
    if out is not None:
        aliases = {len(operands): 0}
        operands.append(out)
        in_specs.append(pl.BlockSpec(memory_space=pl.ANY))
    return pl.pallas_call(
        body,
        grid_spec=pltpu.PrefetchScalarGridSpec(
            num_scalar_prefetch=1,
            grid=(4,),
            in_specs=in_specs,
            out_specs=pl.BlockSpec((rows, BLK), lambda j, order: (0, block_at(order[0], side, j))),
        ),
        out_shape=jax.ShapeDtypeStruct((rows, 16 * BLK), jnp.bfloat16),
        input_output_aliases=aliases,
        compiler_params=params(32),
        cost_estimate=pl.CostEstimate(
            flops=2 * 4 * rows * BLK * width, bytes_accessed=5 * MIB, transcendentals=0
        ),
        name="input_part",
    )(*operands)


def stack_rows(groups, width):
    pieces = [(g, start, piece) for g, group in enumerate(groups) for start, piece in group]

    def body(*refs):
        ins, out, sems = refs[: len(pieces)], refs[-2], refs[-1]
        copies = []
        for k, (g, start, piece) in enumerate(pieces):
            copies.append(
                pltpu.make_async_copy(ins[k], out.at[g, pl.ds(start, piece.shape[0])], sems.at[k])
            )
        for copy in copies:
            copy.start()
        for copy in copies:
            copy.wait()

    return pl.pallas_call(
        body,
        in_specs=[pl.BlockSpec(memory_space=pl.ANY)] * len(pieces),
        out_specs=pl.BlockSpec(memory_space=pl.ANY),
        out_shape=jax.ShapeDtypeStruct((len(groups), BLK, width), jnp.bfloat16),
        scratch_shapes=[pltpu.SemaphoreType.DMA((len(pieces),))],
        cost_estimate=pl.CostEstimate(
            flops=0, bytes_accessed=4 * len(groups) * BLK * width, transcendentals=0
        ),
        name="stack_rows",
    )(*[piece for _, _, piece in pieces])


def add_rows(kept, arrived):
    count, rows, width = kept.shape

    def body(a, b, *outs):
        for k in range(count):
            outs[k][...] = (a[k].astype(jnp.float32) + b[k].astype(jnp.float32)).astype(
                jnp.bfloat16
            )

    return pl.pallas_call(
        body,
        out_shape=[jax.ShapeDtypeStruct((rows, width), jnp.bfloat16)] * count,
        compiler_params=params(24),
        cost_estimate=pl.CostEstimate(
            flops=count * rows * width, bytes_accessed=6 * count * rows * width, transcendentals=0
        ),
        name="add_rows",
    )(kept, arrived)


def sum_columns(kept, first, second, third):
    count, rows, width = kept.shape

    def body(a, b, c, d, *outs):
        for k in range(count):
            total = a[k].astype(jnp.float32) + b[k].astype(jnp.float32)
            total = total + c[k].astype(jnp.float32) + d[k].astype(jnp.float32)
            outs[k][...] = total.astype(jnp.bfloat16)

    return pl.pallas_call(
        body,
        out_shape=[jax.ShapeDtypeStruct((rows, width), jnp.bfloat16)] * count,
        compiler_params=params(24),
        cost_estimate=pl.CostEstimate(
            flops=4 * count * rows * width, bytes_accessed=10 * count * rows * width, transcendentals=0
        ),
        name="sum_columns",
    )(kept, first, second, third)


def finish_rows(own, one, two, three, column, arrived):
    width = own.shape[1]

    def body(a, b, c, d, e, f, out):
        total = a[...].astype(jnp.float32) + b[...].astype(jnp.float32)
        total = total + c[...].astype(jnp.float32) + d[...].astype(jnp.float32)
        out[:PR] = total.astype(jnp.bfloat16)
        out[PR:] = (e[...].astype(jnp.float32) + f[...].astype(jnp.float32)).astype(jnp.bfloat16)

    return pl.pallas_call(
        body,
        out_shape=jax.ShapeDtypeStruct((BLK, width), jnp.bfloat16),
        compiler_params=params(24),
        cost_estimate=pl.CostEstimate(
            flops=4 * BLK * width, bytes_accessed=8 * BLK * width, transcendentals=0
        ),
        name="finish_rows",
    )(own, one, two, three, column, arrived)


def local(
    tokens,
    key_cotangent,
    local_keys,
    pseudo_codes,
    code_exponents,
    outer_weights,
    outer_momentum,
    fragment,
):
    place = lax.axis_index("fsdp")
    here = place.astype(jnp.int32).reshape(1)
    there = here ^ 1

    width = key_cotangent.shape[1]

    own = local_keys[0, local_keys.shape[1] - 1]
    left = to_x(own, 1)
    right = to_x(own, -1)
    peer = to_z(own)
    far = to_x(own, 2)

    theirs = partner_terms(there, tokens, key_cotangent)
    theirs = to_core(theirs)
    zp, kp, x1, x2, x3, kq = own_terms(here, tokens, key_cotangent, theirs)

    peer_q = peer[PR:]
    peer_left_q = to_x(peer_q, 1)
    peer_right_q = to_x(peer_q, -1)
    peer_far_q = to_x(peer_q, 2)
    peer_left_p = to_z(left[:PR])
    peer_right_p = to_z(right[:PR])
    peer_far_p = to_z(far[:PR])
    near = [own, right, far, left]
    near_there = to_core(stack_rows([[(0, block)] for block in near], width))
    across = stack_rows(
        [
            [(0, peer)],
            [(0, peer_right_p), (PR, peer_right_q)],
            [(0, peer_far_p), (PR, peer_far_q)],
            [(0, peer_left_p), (PR, peer_left_q)],
        ],
        width,
    )
    across_there = to_core(across)

    grads = input_part(here, 0, key_cotangent, near, None)
    grads = input_part(there, 0, key_cotangent, [near_there], grads)
    grads = input_part(here, 1, key_cotangent, [across], grads)
    input_grads = input_part(there, 1, key_cotangent, [across_there], grads)

    zp = to_z(zp)
    x1 = to_x(x1, 1)
    x3 = to_x(x3, -1)
    x2 = to_x(x2, 2)
    p0, p1, p2, p3 = add_rows(kp, zp)
    p1 = to_x(p1, 1)
    p3 = to_x(p3, -1)
    p2 = to_x(p2, 2)
    q0, q1 = sum_columns(kq, x1, x2, x3)
    q1 = to_z(q1)
    weight_grads = finish_rows(p0, p1, p2, p3, q0, q1)[None]

    row_count = own.shape[0]
    islands = lax.axis_size("island")
    scales = jnp.exp2(code_exponents[0].astype(jnp.float32))
    scaled_codes = (
        pseudo_codes[0].reshape(row_count, scales.shape[1], -1).astype(jnp.float32)
        * scales[:, :, None]
    )
    island_delta = scaled_codes.reshape(islands, row_count // islands, -1).astype(jnp.bfloat16)
    spread = lax.all_to_all(island_delta, "island", 0, 0, tiled=True)
    part = jnp.sum(spread.astype(jnp.float32), axis=0).astype(jnp.bfloat16)
    part = jnp.broadcast_to(part[None], island_delta.shape)
    total = lax.all_to_all(part, "island", 0, 0, tiled=True).reshape(row_count, -1)
    mean_delta = total.astype(jnp.float32) / islands
    new_momentum = momentum_rate * outer_momentum + mean_delta
    new_weights = outer_weights - outer_rate * (mean_delta + momentum_rate * new_momentum)
    chosen = lax.dynamic_index_in_dim(local_keys[0], fragment[0], 0, keepdims=False)
    synced_keys = (
        keep_share * chosen.astype(jnp.float32) + (1.0 - keep_share) * new_weights
    ).astype(jnp.bfloat16)[None]
    return (input_grads, weight_grads, new_weights, new_momentum, synced_keys)


def solution(mesh):
    placed = (
        P(("island", "fsdp"), None),
        P(("island", "fsdp"), None),
        P("island", None, "fsdp", None),
        P("island", "fsdp", None),
        P("island", "fsdp", None),
        P("fsdp", None),
        P("fsdp", None),
        P("island"),
    )
    return jax.shard_map(
        local,
        mesh=mesh,
        in_specs=placed,
        out_specs=(
            P(("island", "fsdp"), None),
            P("island", "fsdp", None),
            P("fsdp", None),
            P("fsdp", None),
            P("island", "fsdp", None),
        ),
        check_vma=False,
    )
```

time: 204 us -> 296 us (1.45)
  Pallas kernels: 0 us -> 165 us
  waiting for transfers between devices: 154 us -> 53.6 us
  starting transfers between devices: 0.13 us -> 36 us
  matrix products: 24.3 us -> 0 us
  local copies, waits for them, and re-layouts: 2.35 us -> 18.6 us
  between operations: 16.2 us -> 1.55 us
  blocking collectives: 0 us -> 14.1 us
    pallas_call x0 -> x11, Pallas kernels: none -> 165 us  [the longest x2 129 us: stack_rows(): pl.pallas_call(body, in_specs=[pl.BlockSpec(memory_space=pl.ANY)] * len(p...]
    reduce_scatter x1 -> x0, waiting for transfers between devices: 80.8 us -> none  [local(): lax.psum_scatter(jnp.einsum('td,tk->dk', tokens, key_cotangent, preferred...]
    psum x1 -> x0, waiting for transfers between devices: 72.7 us -> none  [local(): lax.psum(island_delta.astype(jnp.bfloat16), 'island').astype(jnp.float32)]
    ppermute x0 -> x21, waiting for transfers between devices: none -> 53.6 us  [the longest x12 26.9 us: to_x(): lax.ppermute(value, 'fsdp', fsdp_perm(lambda h, x, c: (h, x + step, c)))]
    ppermute x0 -> x21, starting transfers between devices: none -> 31.9 us  [the longest x12 18.2 us: to_x(): lax.ppermute(value, 'fsdp', fsdp_perm(lambda h, x, c: (h, x + step, c)))]
    dot_general x2 -> x0, matrix products: 24.3 us -> none  [the longest x1 12.5 us: local(): jnp.einsum('tk,dk->td', key_cotangent, lax.all_gather(key_layer, 'fsdp',...]
    all_to_all x0 -> x1, blocking collectives: none -> 14.1 us  [local(): spread = lax.all_to_all(island_delta, 'island', 0, 0, tiled=True)]
    unnamed x4 -> x50, local copies, waits for them, and re-layouts: 0.01 us -> 10.9 us
  transfers between devices with their start and end apart: 3 -> 22, of which waited for: 2 -> 10; matrix products, arithmetic and copies ran while one was open for 15% -> 5% of each run, Pallas kernels for 0% -> 53%
where the time goes in v1:
time: 296 us; the launch traced here: 294 us
  Pallas kernels  165 us (56%)
  waiting for transfers between devices  53.6 us (18%)
  starting transfers between devices  36 us (12%)
  local copies, waits for them, and re-layouts  18.6 us (6%)
  blocking collectives  14.1 us (5%)
  other arithmetic  6.1 us (2%)
    pallas_call x2, Pallas kernels, stack_rows(): pl.pallas_call(body, in_specs=[pl.BlockSpec(memory_space=pl.ANY)] * len(p...  129 us
    ppermute x12, waiting for transfers between devices, to_x(): lax.ppermute(value, 'fsdp', fsdp_perm(lambda h, x, c: (h, x + step, c)))  26.9 us
    ppermute x6, waiting for transfers between devices, to_z(): return lax.ppermute(value, 'fsdp', fsdp_perm(lambda h, x, c: (h + 1, x, c)))  26.7 us
    ppermute x12, starting transfers between devices, to_x(): lax.ppermute(value, 'fsdp', fsdp_perm(lambda h, x, c: (h, x + step, c)))  18.2 us
    pallas_call x4, Pallas kernels, input_part(): pl.pallas_call(body, grid_spec=pltpu.PrefetchScalarGridSpec(num_scalar_pr...  16.4 us
    all_to_all x1, blocking collectives, local(): spread = lax.all_to_all(island_delta, 'island', 0, 0, tiled=True)  14.1 us
    unnamed x50, local copies, waits for them, and re-layouts  10.9 us
    ppermute x6, starting transfers between devices, to_z(): return lax.ppermute(value, 'fsdp', fsdp_perm(lambda h, x, c: (h + 1, x, c)))  9.91 us
  transfers between devices with their start and end apart: 22, of which 10 were waited for; matrix products, arithmetic and copies ran while one was open for 5% of the time, Pallas kernels for 53%

profile of v1, /device:TPU:1, one launch (start us, length us, event | category | flops | bytes accessed | tf_op | source)
XLA Modules:
  0.0 294.5 jit_solution(2318011264144275631)
XLA Ops:
  2.0 2.8 copy-done.2
  4.8 6.5 %partner_terms.1 = bf16[8,256,1024]{2,1,0:T(8,128)(2,1)} custom-call(s32[1]{0:T(128)S(6)} %xor.3.order_ref, bf16[768,4096]{1,0:T(8,128)(2,1)S(1)} %copy-done.2, bf16[768,1024]{1,0:T(8,128)(2,1)S(1)} %copy-done), custom_call_target="tpu_custom_call" | custom-call | flops 3221225472 | bytes 9437184 | tf_op jit(solution)/shard_map/partner_terms/pallas_call | solution.py:58
  13.9 3.7 %collective-permute-start = (bf16[256,1024]{1,0:T(8,128)(2,1)S(1)}, bf16[256,1024]{1,0:T(8,128)(2,1)S(1)}, u32[]{:S(2)}, u32[]{:S(2)}) collective-permute-start(bf16[256,1024]{1,0:T(8,128)(2,1)S(1)} %slice_bitcast_fusion.refs_0_.rest_0_), channel_id=1, source_target_pairs={{0,8},{1,9},{2,10},{3,11},{4,12},{5,13},{6,14},{7,15},{8,0},{9,1},... | collective-permute-start | bytes 1572872 | tf_op jit(solution)/shard_map/ppermute | solution.py:37
  21.2 8.7 %collective-permute-done.refs_0_ = bf16[256,1024]{1,0:T(8,128)(2,1)S(1)} collective-permute-done((bf16[256,1024]{1,0:T(8,128)(2,1)S(1)}, bf16[256,1024]{1,0:T(8,128)(2,1)S(1)}, u32[]{:S(2)}, u32[]{:S(2)}) %collective-permute-start) | collective-permute-done | bytes 524320 | tf_op jit(solution)/shard_map/ppermute | solution.py:37
  32.5 9.2 %collective-permute-done.1.refs_1_.rest_1_ = bf16[256,1024]{1,0:T(8,128)(2,1)S(1)} collective-permute-done((bf16[256,1024]{1,0:T(8,128)(2,1)S(1)}, bf16[256,1024]{1,0:T(8,128)(2,1)S(1)}, u32[]{:S(2)}, u32[]{:S(2)}) %collective-permute-start.1) | collective-permute-done | bytes 524320 | tf_op jit(solution)/shard_map/ppermute | solution.py:33
  41.7 4.5 %collective-permute-start.9 = (bf16[112,1024]{1,0:T(8,128)(2,1)S(1)}, bf16[112,1024]{1,0:T(8,128)(2,1)}, u32[]{:S(2)}, u32[]{:S(2)}) collective-permute-start(bf16[112,1024]{1,0:T(8,128)(2,1)S(1)} %slice.21), channel_id=1, source_target_pairs={{0,2},{1,3},{2,4},{3,5},{4,6},{5,7},{6,0},{7,1},{8,10},{9,11},{10,... | collective-permute-start | bytes 688136 | tf_op jit(solution)/shard_map/ppermute | solution.py:33
  48.2 64.7 %stack_rows.3 = bf16[4,256,1024]{2,1,0:T(8,128)(2,1)} custom-call(bf16[256,1024]{1,0:T(8,128)(2,1)} %copy-done.4, bf16[256,1024]{1,0:T(8,128)(2,1)} %copy-done.6, bf16[256,1024]{1,0:T(8,128)(2,1)} %copy-done.8, bf16[256,1024]{1,0:T(8,128)(2,1)} %copy-done.10), custom_call_target="tpu_custom_call" | custom-call | bytes 4194304 | tf_op jit(solution)/shard_map/stack_rows/pallas_call | solution.py:187
  119.4 3.0 %collective-permute-start.5 = (bf16[144,1024]{1,0:T(8,128)(2,1)}, bf16[144,1024]{1,0:T(8,128)(2,1)S(1)}, u32[]{:S(2)}, u32[]{:S(2)}) collective-permute-start(bf16[144,1024]{1,0:T(8,128)(2,1)} %slice.22), channel_id=1, source_target_pairs={{0,8},{1,9},{2,10},{3,11},{4,12},{5,13},{6,14},{7,15},{8,0},{9,1},... | collective-permute-start | bytes 884744 | tf_op jit(solution)/shard_map/ppermute | solution.py:37
  124.4 5.3 %collective-permute-done.2.refs_1_ = bf16[144,1024]{1,0:T(8,128)(2,1)S(1)} collective-permute-done((bf16[144,1024]{1,0:T(8,128)(2,1)}, bf16[144,1024]{1,0:T(8,128)(2,1)S(1)}, u32[]{:S(2)}, u32[]{:S(2)}) %collective-permute-start.2) | collective-permute-done | bytes 294944 | tf_op jit(solution)/shard_map/ppermute | solution.py:37
  129.8 6.3 %collective-permute-done.5.refs_3_ = bf16[144,1024]{1,0:T(8,128)(2,1)S(1)} collective-permute-done((bf16[144,1024]{1,0:T(8,128)(2,1)}, bf16[144,1024]{1,0:T(8,128)(2,1)S(1)}, u32[]{:S(2)}, u32[]{:S(2)}) %collective-permute-start.5) | collective-permute-done | bytes 294944 | tf_op jit(solution)/shard_map/ppermute | solution.py:37
  136.1 6.3 %collective-permute-done.8.refs_5_ = bf16[144,1024]{1,0:T(8,128)(2,1)S(1)} collective-permute-done((bf16[144,1024]{1,0:T(8,128)(2,1)}, bf16[144,1024]{1,0:T(8,128)(2,1)S(1)}, u32[]{:S(2)}, u32[]{:S(2)}) %collective-permute-start.8) | collective-permute-done | bytes 294944 | tf_op jit(solution)/shard_map/ppermute | solution.py:37
  143.1 64.7 %stack_rows.2.rest_0_ = bf16[4,256,1024]{2,1,0:T(8,128)(2,1)} custom-call(bf16[256,1024]{1,0:T(8,128)(2,1)} %copy-done.19, bf16[144,1024]{1,0:T(8,128)(2,1)} %copy-done.21, bf16[112,1024]{1,0:T(8,128)(2,1)} %collective-permute-done.3.refs_2_, bf16[144,1024]{1,0:T(8,128)(2,1)} %copy-done.22, bf16[112,1024]{1,0:T(8,128)(2,1)} %collective-permute-done.6.refs_4_, ...), custom_call_target="tpu_custom_call" | custom-call | bytes 4194304 | tf_op jit(solution)/shard_map/stack_rows/pallas_call | solution.py:187
  208.9 14.1 %all_to_all.10 = bf16[8,32,1024]{2,1,0:T(8,128)(2,1)S(1)} all-to-all(bf16[8,32,1024]{2,1,0:T(8,128)(2,1)S(1)} %multiply_convert_fusion), channel_id=1, replica_groups=mesh['island'=8,'fsdp'=16] {'island'}, dimensions={0} | all-to-all | bytes 1048576 | tf_op jit(solution)/shard_map/all_to_all | solution.py:331
  223.9 4.1 %all-to-all-start.1 = ((bf16[8,32,1024]{2,1,0:T(8,128)(2,1)}), bf16[8,32,1024]{2,1,0:T(8,128)(2,1)}, u32[]{:S(2)}, u32[]{:S(2)}) async-start(bf16[8,32,1024]{2,1,0:T(8,128)(2,1)} %broadcast_in_dim.14), calls=%async_computation.1 | async-start | bytes 1048576 | tf_op jit(solution)/shard_map/all_to_all | solution.py:334
  228.1 9.5 %own_terms.1 = (bf16[4,144,1024]{2,1,0:T(8,128)(2,1)}, bf16[4,144,1024]{2,1,0:T(8,128)(2,1)S(1)}, bf16[2,112,1024]{2,1,0:T(8,128)(2,1)S(1)}, bf16[2,112,1024]{2,...) custom-call(s32[1]{0:T(128)} %bitcast.order_ref, bf16[768,4096]{1,0:T(8,128)(2,1)} %tok_ref.3, ...), custom_call_target="tpu_custom_call" | custom-call | flops 3221225472 | bytes 13631488 | tf_op jit(solution)/shard_map/own_terms/pallas_call | solution.py:97
  244.3 3.4 %input_part.4.rest_1_ = bf16[768,4096]{1,0:T(8,128)(2,1)} custom-call(s32[1]{0:T(128)} %bitcast.order_ref, bf16[768,1024]{1,0:T(8,128)(2,1)S(1)} %copy-done.1, bf16[256,1024]{1,0:T(8,128)(2,1)S(1)} %copy-done.5, bf16[256,1024]{1,0:T(8,128)(2,1)S(1)} %copy-done.7, bf16[256,1024]{1,0:T(8,128)(2,1)S(1)} %copy-done.9, bf16[256,1024]{1,0:T(8,128)(2,1)S(1)} %copy-done.11), custom_call_target="tpu_custom_call" | custom-call | flops 1610612736 | bytes 5242880 | tf_op jit(solution)/shard_map/input_part/pallas_call | solution.py:154
  252.0 3.3 %fusion.4 = (bf16[1,256,1024]{2,1,0:T(8,128)(2,1)}, f32[256,1024]{1,0:T(8,128)}, f32[256,1024]{1,0:T(8,128)}) fusion(bf16[1,4,256,1024]{3,2,1,0:T(8,128)(2,1)} %param.10, s32[]{:T(128)S(6)} %select_n.4, f32[256,1024]{1,0:T(8,128)S(1)} %copy-done.20, f32[8,32,1024]{2,1,0:T(8,128)S(1)} %convert_multiply_fusion, f32[256,1024]{1,0:T(8,128)} %param.14), kind=kLoop, calls=%fused_computation.9 | loop fusion | flops 2621440 | bytes 6291460 | tf_op jit(solution)/shard_map/broadcast_in_dim | solution.py:339
  255.3 4.9 %input_part.5.rest_1_ = bf16[768,4096]{1,0:T(8,128)(2,1)} custom-call(s32[1]{0:T(128)S(6)} %xor.3.order_ref, bf16[768,1024]{1,0:T(8,128)(2,1)S(1)} %copy-done.1, bf16[4,256,1024]{2,1,0:T(8,128)(2,1)} %collective-permute-done.11.rest_0_, bf16[768,4096]{1,0:T(8,128)(2,1)} %input_part.4.rest_1_), custom_call_target="tpu_custom_call", output_to_operand_aliasing={{}: (3, {})} | custom-call | flops 1610612736 | bytes 5242880 | tf_op jit(solution)/shard_map/input_part/pallas_call | solution.py:154
  262.8 6.4 %collective-permute-done.18.c = bf16[2,112,1024]{2,1,0:T(8,128)(2,1)S(1)} collective-permute-done((bf16[2,112,1024]{2,1,0:T(8,128)(2,1)}, bf16[2,112,1024]{2,1,0:T(8,128)(2,1)S(1)}, u32[]{:S(2)}, u32[]{:S(2)}) %collective-permute-start.18) | collective-permute-done | bytes 458784 | tf_op jit(solution)/shard_map/ppermute | solution.py:33
  269.3 3.1 %collective-permute-done.19.d = bf16[2,112,1024]{2,1,0:T(8,128)(2,1)S(1)} collective-permute-done((bf16[2,112,1024]{2,1,0:T(8,128)(2,1)}, bf16[2,112,1024]{2,1,0:T(8,128)(2,1)S(1)}, u32[]{:S(2)}, u32[]{:S(2)}) %collective-permute-start.19) | collective-permute-done | bytes 458784 | tf_op jit(solution)/shard_map/ppermute | solution.py:33
  277.6 3.3 %collective-permute-start.15 = (bf16[144,1024]{1,0:T(8,128)(2,1)S(1)}, bf16[144,1024]{1,0:T(8,128)(2,1)S(1)}, u32[]{:S(2)}, u32[]{:S(2)}) collective-permute-start(bf16[144,1024]{1,0:T(8,128)(2,1)S(1)} %get-tuple-element.21), channel_id=1, source_target_pairs={{0,4},{1,5},{2,6},{3,7},{4,0},{5,1},{6,2},{7,3},{8,12},{9,13},{10,... | collective-permute-start | bytes 884744 | tf_op jit(solution)/shard_map/ppermute | solution.py:33
  280.9 3.3 %input_part.6.rest_1_ = bf16[768,4096]{1,0:T(8,128)(2,1)} custom-call(s32[1]{0:T(128)} %bitcast.order_ref, bf16[768,1024]{1,0:T(8,128)(2,1)S(1)} %copy-done.1, bf16[4,256,1024]{2,1,0:T(8,128)(2,1)S(1)} %copy-done.3, bf16[768,4096]{1,0:T(8,128)(2,1)} %input_part.5.rest_1_), custom_call_target="tpu_custom_call", output_to_operand_aliasing={{}: (3, {})} | custom-call | flops 1610612736 | bytes 5242880 | tf_op jit(solution)/shard_map/input_part/pallas_call | solution.py:154
  284.2 4.9 %input_part.7 = bf16[768,4096]{1,0:T(8,128)(2,1)} custom-call(s32[1]{0:T(128)S(6)} %xor.3.order_ref, bf16[768,1024]{1,0:T(8,128)(2,1)S(1)} %copy-done.1, bf16[4,256,1024]{2,1,0:T(8,128)(2,1)} %collective-permute-done.10.rest_0_, bf16[768,4096]{1,0:T(8,128)(2,1)} %input_part.6.rest_1_), custom_call_target="tpu_custom_call", output_to_operand_aliasing={{}: (3, {})} | custom-call | flops 1610612736 | bytes 5242880 | tf_op jit(solution)/shard_map/input_part/pallas_call | solution.py:154
  289.1 4.4 %collective-permute-done.15.c = bf16[144,1024]{1,0:T(8,128)(2,1)S(1)} collective-permute-done((bf16[144,1024]{1,0:T(8,128)(2,1)S(1)}, bf16[144,1024]{1,0:T(8,128)(2,1)S(1)}, u32[]{:S(2)}, u32[]{:S(2)}) %collective-permute-start.15) | collective-permute-done | bytes 294944 | tf_op jit(solution)/shard_map/ppermute | solution.py:33
  (97 shorter events, 42.5 us)
Async XLA Ops:
  11.4 216.7 %collective-permute-start.12 = (bf16[8,256,1024]{2,1,0:T(8,128)(2,1)}, bf16[8,256,1024]{2,1,0:T(8,128)(2,1)}, u32[]{:S(2)}, u32[]{:S(2)}) collective-permute-start(bf16[8,256,1024]{2,1,0:T(8,128)(2,1)} %partner_terms.1), channel_id=1, source_target_pairs={{0,1},{1,0},{2,3},{3,2},{4,5},{5,4},{6,7},{7,6},{8,9},{9,8},{10,11... | collective-permute-start | bytes 12582920 | tf_op jit(solution)/shard_map/ppermute | solution.py:41
  13.9 16.0 %collective-permute-start = (bf16[256,1024]{1,0:T(8,128)(2,1)S(1)}, bf16[256,1024]{1,0:T(8,128)(2,1)S(1)}, u32[]{:S(2)}, u32[]{:S(2)}) collective-permute-start(bf16[256,1024]{1,0:T(8,128)(2,1)S(1)} %slice_bitcast_fusion.refs_0_.rest_0_), channel_id=1, source_target_pairs={{0,8},{1,9},{2,10},{3,11},{4,12},{5,13},{6,14},{7,15},{8,0},{9,1},... | collective-permute-start | bytes 1572872 | tf_op jit(solution)/shard_map/ppermute | solution.py:37
  17.6 24.1 %collective-permute-start.1 = (bf16[256,1024]{1,0:T(8,128)(2,1)S(1)}, bf16[256,1024]{1,0:T(8,128)(2,1)S(1)}, u32[]{:S(2)}, u32[]{:S(2)}) collective-permute-start(bf16[256,1024]{1,0:T(8,128)(2,1)S(1)} %slice_bitcast_fusion.refs_0_.rest_0_), channel_id=1, source_target_pairs={{0,6},{1,7},{2,0},{3,1},{4,2},{5,3},{6,4},{7,5},{8,14},{9,15},{10,... | collective-permute-start | bytes 1572872 | tf_op jit(solution)/shard_map/ppermute | solution.py:33
  20.1 21.6 %collective-permute-start.4 = (bf16[256,1024]{1,0:T(8,128)(2,1)S(1)}, bf16[256,1024]{1,0:T(8,128)(2,1)S(1)}, u32[]{:S(2)}, u32[]{:S(2)}) collective-permute-start(bf16[256,1024]{1,0:T(8,128)(2,1)S(1)} %slice_bitcast_fusion.refs_0_.rest_0_), channel_id=1, source_target_pairs={{0,4},{1,5},{2,6},{3,7},{4,0},{5,1},{6,2},{7,3},{8,12},{9,13},{10,... | collective-permute-start | bytes 1572872 | tf_op jit(solution)/shard_map/ppermute | solution.py:33
  20.6 26.7 %collective-permute-start.7 = (bf16[256,1024]{1,0:T(8,128)(2,1)S(1)}, bf16[256,1024]{1,0:T(8,128)(2,1)S(1)}, u32[]{:S(2)}, u32[]{:S(2)}) collective-permute-start(bf16[256,1024]{1,0:T(8,128)(2,1)S(1)} %slice_bitcast_fusion.refs_0_.rest_0_), channel_id=1, source_target_pairs={{0,2},{1,3},{2,4},{3,5},{4,6},{5,7},{6,0},{7,1},{8,10},{9,11},{10,... | collective-permute-start | bytes 1572872 | tf_op jit(solution)/shard_map/ppermute | solution.py:33
  29.9 112.5 %copy-start.19 = (bf16[256,1024]{1,0:T(8,128)(2,1)}, bf16[256,1024]{1,0:T(8,128)(2,1)S(1)}, u32[]{:S(2)}) copy-start(bf16[256,1024]{1,0:T(8,128)(2,1)S(1)} %collective-permute-done.refs_0_) | copy-start | bytes 1572868
  29.9 92.6 %copy-start.24 = (s32[1,256,8]{1,2,0:T(8,128)S(1)}, s32[1,256,8]{1,2,0:T(8,128)}, u32[]{:S(2)}) copy-start(s32[1,256,8]{1,2,0:T(8,128)} %param.12) | copy-start | bytes 24580
  29.9 89.5 %collective-permute-start.3 = (bf16[112,1024]{1,0:T(8,128)(2,1)S(1)}, bf16[112,1024]{1,0:T(8,128)(2,1)}, u32[]{:S(2)}, u32[]{:S(2)}) collective-permute-start(bf16[112,1024]{1,0:T(8,128)(2,1)S(1)} %slice.21), channel_id=1, source_target_pairs={{0,6},{1,7},{2,0},{3,1},{4,2},{5,3},{6,4},{7,5},{8,14},{9,15},{10,... | collective-permute-start | bytes 688136 | tf_op jit(solution)/shard_map/ppermute | solution.py:33
  41.7 77.7 %collective-permute-start.6 = (bf16[112,1024]{1,0:T(8,128)(2,1)S(1)}, bf16[112,1024]{1,0:T(8,128)(2,1)}, u32[]{:S(2)}, u32[]{:S(2)}) collective-permute-start(bf16[112,1024]{1,0:T(8,128)(2,1)S(1)} %slice.21), channel_id=1, source_target_pairs={{0,4},{1,5},{2,6},{3,7},{4,0},{5,1},{6,2},{7,3},{8,12},{9,13},{10,... | collective-permute-start | bytes 688136 | tf_op jit(solution)/shard_map/ppermute | solution.py:33
  41.7 80.7 %collective-permute-start.9 = (bf16[112,1024]{1,0:T(8,128)(2,1)S(1)}, bf16[112,1024]{1,0:T(8,128)(2,1)}, u32[]{:S(2)}, u32[]{:S(2)}) collective-permute-start(bf16[112,1024]{1,0:T(8,128)(2,1)S(1)} %slice.21), channel_id=1, source_target_pairs={{0,2},{1,3},{2,4},{3,5},{4,6},{5,7},{6,0},{7,1},{8,10},{9,11},{10,... | collective-permute-start | bytes 688136 | tf_op jit(solution)/shard_map/ppermute | solution.py:33
  112.8 137.1 %collective-permute-start.11 = (bf16[4,256,1024]{2,1,0:T(8,128)(2,1)}, bf16[4,256,1024]{2,1,0:T(8,128)(2,1)}, u32[]{:S(2)}, u32[]{:S(2)}) collective-permute-start(bf16[4,256,1024]{2,1,0:T(8,128)(2,1)} %stack_rows.3), channel_id=1, source_target_pairs={{0,1},{1,0},{2,3},{3,2},{4,5},{5,4},{6,7},{7,6},{8,9},{9,8},{10,11... | collective-permute-start | bytes 6291464 | tf_op jit(solution)/shard_map/ppermute | solution.py:41
  119.4 10.4 %collective-permute-start.2 = (bf16[144,1024]{1,0:T(8,128)(2,1)}, bf16[144,1024]{1,0:T(8,128)(2,1)S(1)}, u32[]{:S(2)}, u32[]{:S(2)}) collective-permute-start(bf16[144,1024]{1,0:T(8,128)(2,1)} %slice.20), channel_id=1, source_target_pairs={{0,8},{1,9},{2,10},{3,11},{4,12},{5,13},{6,14},{7,15},{8,0},{9,1},... | collective-permute-start | bytes 884744 | tf_op jit(solution)/shard_map/ppermute | solution.py:37
  119.4 16.7 %collective-permute-start.5 = (bf16[144,1024]{1,0:T(8,128)(2,1)}, bf16[144,1024]{1,0:T(8,128)(2,1)S(1)}, u32[]{:S(2)}, u32[]{:S(2)}) collective-permute-start(bf16[144,1024]{1,0:T(8,128)(2,1)} %slice.22), channel_id=1, source_target_pairs={{0,8},{1,9},{2,10},{3,11},{4,12},{5,13},{6,14},{7,15},{8,0},{9,1},... | collective-permute-start | bytes 884744 | tf_op jit(solution)/shard_map/ppermute | solution.py:37
  122.4 20.0 %collective-permute-start.8 = (bf16[144,1024]{1,0:T(8,128)(2,1)}, bf16[144,1024]{1,0:T(8,128)(2,1)S(1)}, u32[]{:S(2)}, u32[]{:S(2)}) collective-permute-start(bf16[144,1024]{1,0:T(8,128)(2,1)} %slice.23), channel_id=1, source_target_pairs={{0,8},{1,9},{2,10},{3,11},{4,12},{5,13},{6,14},{7,15},{8,0},{9,1},... | collective-permute-start | bytes 884744 | tf_op jit(solution)/shard_map/ppermute | solution.py:37
  207.8 76.4 %collective-permute-start.10 = (bf16[4,256,1024]{2,1,0:T(8,128)(2,1)}, bf16[4,256,1024]{2,1,0:T(8,128)(2,1)}, u32[]{:S(2)}, u32[]{:S(2)}) collective-permute-start(bf16[4,256,1024]{2,1,0:T(8,128)(2,1)} %stack_rows.2.rest_0_), channel_id=1, source_target_pairs={{0,1},{1,0},{2,3},{3,2},{4,5},{5,4},{6,7},{7,6},{8,9},{9,8},{10,11... | collective-permute-start | bytes 6291464 | tf_op jit(solution)/shard_map/ppermute | solution.py:41
  223.9 23.8 %all-to-all-start.1 = ((bf16[8,32,1024]{2,1,0:T(8,128)(2,1)}), bf16[8,32,1024]{2,1,0:T(8,128)(2,1)}, u32[]{:S(2)}, u32[]{:S(2)}) async-start(bf16[8,32,1024]{2,1,0:T(8,128)(2,1)} %broadcast_in_dim.14), calls=%async_computation.1 | async-start | bytes 1048576 | tf_op jit(solution)/shard_map/all_to_all | solution.py:334
  241.7 33.1 %collective-permute-start.13 = (bf16[4,144,1024]{2,1,0:T(8,128)(2,1)}, bf16[4,144,1024]{2,1,0:T(8,128)(2,1)}, u32[]{:S(2)}, u32[]{:S(2)}) collective-permute-start(bf16[4,144,1024]{2,1,0:T(8,128)(2,1)} %get-tuple-element.18), channel_id=1, source_target_pairs={{0,8},{1,9},{2,10},{3,11},{4,12},{5,13},{6,14},{7,15},{8,0},{9,1},... | collective-permute-start | bytes 3538952 | tf_op jit(solution)/shard_map/ppermute | solution.py:37
  248.9 13.9 %collective-permute-start.17 = (bf16[2,112,1024]{2,1,0:T(8,128)(2,1)}, bf16[2,112,1024]{2,1,0:T(8,128)(2,1)S(1)}, u32[]{:S(2)}, u32[]{:S(2)}) collective-permute-start(bf16[2,112,1024]{2,1,0:T(8,128)(2,1)} %copy-done.18), channel_id=1, source_target_pairs={{0,2},{1,3},{2,4},{3,5},{4,6},{5,7},{6,0},{7,1},{8,10},{9,11},{10,... | collective-permute-start | bytes 1376264 | tf_op jit(solution)/shard_map/ppermute | solution.py:33
  249.5 19.8 %collective-permute-start.18 = (bf16[2,112,1024]{2,1,0:T(8,128)(2,1)}, bf16[2,112,1024]{2,1,0:T(8,128)(2,1)S(1)}, u32[]{:S(2)}, u32[]{:S(2)}) collective-permute-start(bf16[2,112,1024]{2,1,0:T(8,128)(2,1)} %copy-done.17), channel_id=1, source_target_pairs={{0,4},{1,5},{2,6},{3,7},{4,0},{5,1},{6,2},{7,3},{8,12},{9,13},{10,... | collective-permute-start | bytes 1376264 | tf_op jit(solution)/shard_map/ppermute | solution.py:33
  250.0 22.4 %collective-permute-start.19 = (bf16[2,112,1024]{2,1,0:T(8,128)(2,1)}, bf16[2,112,1024]{2,1,0:T(8,128)(2,1)S(1)}, u32[]{:S(2)}, u32[]{:S(2)}) collective-permute-start(bf16[2,112,1024]{2,1,0:T(8,128)(2,1)} %copy-done.16), channel_id=1, source_target_pairs={{0,6},{1,7},{2,0},{3,1},{4,2},{5,3},{6,4},{7,5},{8,14},{9,15},{10,... | collective-permute-start | bytes 1376264 | tf_op jit(solution)/shard_map/ppermute | solution.py:33
  272.6 16.5 %collective-permute-start.20 = (bf16[112,1024]{1,0:T(8,128)(2,1)S(1)}, bf16[112,1024]{1,0:T(8,128)(2,1)S(1)}, u32[]{:S(2)}, u32[]{:S(2)}) collective-permute-start(bf16[112,1024]{1,0:T(8,128)(2,1)S(1)} %get-tuple-element.28), channel_id=1, source_target_pairs={{0,8},{1,9},{2,10},{3,11},{4,12},{5,13},{6,14},{7,15},{8,0},{9,1},... | collective-permute-start | bytes 688136 | tf_op jit(solution)/shard_map/ppermute | solution.py:37
  276.3 12.7 %collective-permute-start.14 = (bf16[144,1024]{1,0:T(8,128)(2,1)S(1)}, bf16[144,1024]{1,0:T(8,128)(2,1)S(1)}, u32[]{:S(2)}, u32[]{:S(2)}) collective-permute-start(bf16[144,1024]{1,0:T(8,128)(2,1)S(1)} %get-tuple-element.20), channel_id=1, source_target_pairs={{0,2},{1,3},{2,4},{3,5},{4,6},{5,7},{6,0},{7,1},{8,10},{9,11},{10,... | collective-permute-start | bytes 884744 | tf_op jit(solution)/shard_map/ppermute | solution.py:33
  277.6 15.9 %collective-permute-start.15 = (bf16[144,1024]{1,0:T(8,128)(2,1)S(1)}, bf16[144,1024]{1,0:T(8,128)(2,1)S(1)}, u32[]{:S(2)}, u32[]{:S(2)}) collective-permute-start(bf16[144,1024]{1,0:T(8,128)(2,1)S(1)} %get-tuple-element.21), channel_id=1, source_target_pairs={{0,4},{1,5},{2,6},{3,7},{4,0},{5,1},{6,2},{7,3},{8,12},{9,13},{10,... | collective-permute-start | bytes 884744 | tf_op jit(solution)/shard_map/ppermute | solution.py:33
  280.9 12.6 %collective-permute-start.16 = (bf16[144,1024]{1,0:T(8,128)(2,1)S(1)}, bf16[144,1024]{1,0:T(8,128)(2,1)S(1)}, u32[]{:S(2)}, u32[]{:S(2)}) collective-permute-start(bf16[144,1024]{1,0:T(8,128)(2,1)S(1)} %get-tuple-element.22), channel_id=1, source_target_pairs={{0,6},{1,7},{2,0},{3,1},{4,2},{5,3},{6,4},{7,5},{8,14},{9,15},{10,... | collective-permute-start | bytes 884744 | tf_op jit(solution)/shard_map/ppermute | solution.py:33
  (23 other events, 183.9 us)

commit v2 on v0

v2 whole, which is shorter than its diff:
```python
import jax
import jax.numpy as jnp
from jax import lax
from jax.experimental import pallas as pl
from jax.experimental.pallas import tpu as pltpu
from jax.sharding import PartitionSpec as P

momentum_rate = 0.9
outer_rate = 0.7
keep_share = 0.5

ISLANDS = 8
BLK = 256
MIB = 1 << 20
TERM_MIB = 58
INPUT_MIB = 24
COST = 0.3


def fsdp_perm(move):
    pairs = []
    for h in range(2):
        for x in range(4):
            for c in range(2):
                h2, x2, c2 = move(h, x, c)
                pairs.append((h * 8 + x * 2 + c, (h2 % 2) * 8 + (x2 % 4) * 2 + c2))
    return pairs


def block_at(place, dh, dx):
    return (place ^ (dh << 3)) & 9 | ((((place >> 1) + dx) & 3) << 1)


def to_x(value, step):
    return lax.ppermute(value, "fsdp", fsdp_perm(lambda h, x, c: (h, x + step, c)))


def to_z(value):
    return lax.ppermute(value, "fsdp", fsdp_perm(lambda h, x, c: (h + 1, x, c)))


def to_island(value, move):
    pairs = []
    for y in range(4):
        for side in range(2):
            y2, side2 = move(y, side)
            pairs.append((y * 2 + side, (y2 % 4) * 2 + side2))
    return lax.ppermute(value, "island", pairs)


def to_y(value, step):
    return to_island(value, lambda y, side: (y + step, side))


def to_side(value):
    return to_island(value, lambda y, side: (y, 1 - side))


def to_core(value):
    return lax.ppermute(value, "fsdp", fsdp_perm(lambda h, x, c: (h, x, 1 - c)))


def after(value, earlier):
    return lax.optimization_barrier((value, earlier))[0]


def phase(*values):
    return lax.optimization_barrier(values)


def cost(flops, size):
    return pl.CostEstimate(
        flops=int(flops * COST), bytes_accessed=int(size * COST), transcendentals=0
    )


def params(mib):
    return pltpu.CompilerParams(vmem_limit_bytes=mib * MIB)


def term(tok, kc):
    return lax.dot_general(tok, kc, (((0,), (0,)), ((), ())), preferred_element_type=jnp.float32)


def chip_terms(order, side, tokens, kc, their_tokens, their_kc):
    rows, width = kc.shape

    def body(order_ref, tok_ref, kc_ref, their_tok_ref, their_kc_ref, *rest):
        outs, held, sems = rest[:4], rest[4], rest[5]
        j = pl.program_id(0)
        total = term(tok_ref[...], kc_ref[...])
        total += term(their_tok_ref[...], their_kc_ref[...])
        total = total.astype(jnp.bfloat16)
        for k in range(4):

            @pl.when(j == k)
            def _():
                held[k] = total
                pltpu.make_async_copy(held.at[k], outs[k], sems.at[k]).start()

        @pl.when(j == 3)
        def _():
            for k in range(4):
                pltpu.make_async_copy(held.at[k], outs[k], sems.at[k]).wait()

    whole = pl.BlockSpec((rows, width), lambda j, order: (0, 0))
    columns = pl.BlockSpec((rows, BLK), lambda j, order: (0, block_at(order[0], side, j)))
    return pl.pallas_call(
        body,
        grid_spec=pltpu.PrefetchScalarGridSpec(
            num_scalar_prefetch=1,
            grid=(4,),
            in_specs=[columns, whole, columns, whole],
            out_specs=[pl.BlockSpec(memory_space=pl.ANY)] * 4,
            scratch_shapes=[
                pltpu.VMEM((4, BLK, width), jnp.bfloat16),
                pltpu.SemaphoreType.DMA((4,)),
            ],
        ),
        out_shape=[jax.ShapeDtypeStruct((BLK, width), jnp.bfloat16)] * 4,
        compiler_params=params(TERM_MIB),
        cost_estimate=cost(2 * 8 * rows * BLK * width, 12 * MIB),
        name="chip_terms",
    )(order, tokens, kc, their_tokens, their_kc)


def walk(j):
    return j ^ (j >> 1)


def side_products(order, side, first, kc, their_kc, blocks, grads):
    rows, width = kc.shape
    count = len(blocks)

    def body(order_ref, kc_ref, their_kc_ref, *rest):
        out_ref, theirs_ref = rest[-2:]
        j = pl.program_id(0)
        for k in range(count):

            @pl.when(j == k)
            def _():
                block = rest[k][...]
                for kc_rows, ref in ((kc_ref, out_ref), (their_kc_ref, theirs_ref.at[0])):
                    ref[...] = lax.dot_general(
                        kc_rows[...],
                        block,
                        (((1,), (1,)), ((), ())),
                        preferred_element_type=jnp.float32,
                    ).astype(jnp.bfloat16)

    def whole(shape):
        return pl.BlockSpec(shape, lambda j, order: (0,) * len(shape))

    operands = [order, kc, their_kc, *blocks]
    in_specs = [whole((rows, width))] * 2 + [whole((BLK, width))] * count
    aliases = {}
    if grads is not None:
        aliases = {len(operands): 0}
        operands.append(grads)
        in_specs.append(pl.BlockSpec(memory_space=pl.ANY))
    return pl.pallas_call(
        body,
        grid_spec=pltpu.PrefetchScalarGridSpec(
            num_scalar_prefetch=1,
            grid=(count,),
            in_specs=in_specs,
            out_specs=[
                pl.BlockSpec(
                    (rows, BLK), lambda j, order: (0, block_at(order[0], side, walk(first + j)))
                ),
                pl.BlockSpec((1, rows, BLK), lambda j, order: (j, 0, 0)),
            ],
        ),
        out_shape=[
            jax.ShapeDtypeStruct((rows, 16 * BLK), jnp.bfloat16),
            jax.ShapeDtypeStruct((count, rows, BLK), jnp.bfloat16),
        ],
        input_output_aliases=aliases,
        compiler_params=params(INPUT_MIB),
        cost_estimate=cost(4 * count * rows * BLK * width, 2 * count * MIB),
        name="side_products",
    )(*operands)


def put_blocks(order, grads, *arrived):
    counts = [part.shape[0] for part in arrived]
    pieces = [(group, k) for group, count in enumerate(counts) for k in range(count)]

    def body(order_ref, *rest):
        out_ref, sems = rest[-2:]
        copies = []
        for n, (group, k) in enumerate(pieces):
            place = block_at(order_ref[0] ^ 1, n // 4, walk(n % 4))
            copies.append(
                pltpu.make_async_copy(
                    rest[group].at[k],
                    out_ref.at[:, pl.ds(pl.multiple_of(place * BLK, BLK), BLK)],
                    sems.at[n],
                )
            )
        for copy in copies:
            copy.start()
        for copy in copies:
            copy.wait()

    return pl.pallas_call(
        body,
        grid_spec=pltpu.PrefetchScalarGridSpec(
            num_scalar_prefetch=1,
            grid=(1,),
            in_specs=[
                *[pl.BlockSpec(part.shape, lambda j, order: (0, 0, 0)) for part in arrived],
                pl.BlockSpec(memory_space=pl.ANY),
            ],
            out_specs=pl.BlockSpec(memory_space=pl.ANY),
            scratch_shapes=[pltpu.SemaphoreType.DMA((len(pieces),))],
        ),
        out_shape=jax.ShapeDtypeStruct(grads.shape, jnp.bfloat16),
        input_output_aliases={1 + len(arrived): 0},
        compiler_params=params(INPUT_MIB),
        cost_estimate=cost(0, 6 * MIB),
        name="put_blocks",
    )(order, *arrived, grads)


def dequantize(codes, exponents):
    rows, blocks = exponents.shape
    size = codes.shape[1] // blocks

    def body(codes_ref, exponents_ref, out_ref):
        scales = jnp.exp2(exponents_ref[...].astype(jnp.float32))
        for k in range(blocks):
            part = codes_ref[:, k * size : (k + 1) * size].astype(jnp.float32)
            out_ref[:, k * size : (k + 1) * size] = (part * scales[:, k : k + 1]).astype(
                jnp.bfloat16
            )

    return pl.pallas_call(
        body,
        out_shape=jax.ShapeDtypeStruct(codes.shape, jnp.bfloat16),
        compiler_params=params(INPUT_MIB),
        cost_estimate=cost(2 * rows * codes.shape[1], 2 * MIB),
        name="dequantize",
    )(codes, exponents)


def add_blocks(*blocks):
    rows, width = blocks[0].shape
    step = rows // 2

    def body(*refs):
        total = refs[0][...].astype(jnp.float32)
        for ref in refs[1:-1]:
            total = total + ref[...].astype(jnp.float32)
        refs[-1][...] = total.astype(jnp.bfloat16)

    spec = pl.BlockSpec((step, width), lambda j: (j, 0))
    return pl.pallas_call(
        body,
        grid=(2,),
        in_specs=[spec] * len(blocks),
        out_specs=spec,
        out_shape=jax.ShapeDtypeStruct((rows, width), jnp.bfloat16),
        compiler_params=params(INPUT_MIB),
        cost_estimate=cost(len(blocks) * rows * width, 2 * (len(blocks) + 1) * rows * width),
        name="add_blocks",
    )(*blocks)


def local(
    tokens,
    key_cotangent,
    local_keys,
    pseudo_codes,
    code_exponents,
    outer_weights,
    outer_momentum,
    fragment,
):
    place = lax.axis_index("fsdp")
    here = place.astype(jnp.int32).reshape(1)

    own = local_keys[0, local_keys.shape[1] - 1]
    their_kc = to_core(key_cotangent)
    their_tokens = to_core(tokens)
    left = to_x(own, 1)
    right = to_x(own, -1)
    peer = to_z(own)
    delta = dequantize(pseudo_codes[0], after(code_exponents[0], own))
    far = to_x(after(own, (delta, their_kc)), 2)
    other_delta = to_side(delta)

    away = chip_terms(here, 1, tokens, key_cotangent, their_tokens, after(their_kc, delta))
    left, right, peer, delta = after((left, right, peer, delta), away[0])

    away_one = to_x(away[1], 1)
    away_three = to_x(away[3], -1)
    peer_left = to_z(left)
    home = chip_terms(here, 0, tokens, key_cotangent, their_tokens, after(their_kc, (peer, right)))
    pair = add_blocks(after(delta, home[0]), other_delta)
    away, away_one, away_three, peer_left, pair, home, far, own, right = phase(
        away, away_one, away_three, peer_left, pair, home, far, own, right
    )

    away_two = to_x(away[2], 2)
    peer_right = to_z(right)
    pair_next = to_y(pair, 1)
    pair_last = to_y(pair, -1)
    near = [own, right, left, far]
    grads, near_theirs = side_products(here, 0, 0, key_cotangent, their_kc, near, None)
    away, away_two, peer_right, pair, pair_next, pair_last, grads, near_theirs, home, far = phase(
        away, away_two, peer_right, pair, pair_next, pair_last, grads, near_theirs, home, far
    )

    home_one = to_x(home[1], 1)
    home_three = to_x(home[3], -1)
    peer_far = to_z(far)
    near_there = to_core(near_theirs)
    pair_far = to_y(pair, 2)
    away_sum = add_blocks(away[0], away_one, away_two, away_three)
    across = after([peer, peer_right, peer_left], away_sum)
    grads, across_theirs = side_products(here, 1, 0, key_cotangent, their_kc, across, grads)
    home_one, home_three, peer_far, near_there, pair_far, away_sum, grads, across_theirs, home = phase(
        home_one, home_three, peer_far, near_there, pair_far, away_sum, grads, across_theirs, home
    )

    home_two = to_x(home[2], 2)
    crossed = to_z(away_sum)
    across_there = to_core(across_theirs)
    grads, last_theirs = side_products(here, 1, 3, key_cotangent, their_kc, [peer_far], grads)
    last_there = to_core(last_theirs)
    pairs = (after(pair, grads), pair_next, pair_last, pair_far)
    mean_delta = sum(part.astype(jnp.float32) for part in pairs) / ISLANDS
    new_momentum = momentum_rate * outer_momentum + mean_delta
    new_weights = outer_weights - outer_rate * (mean_delta + momentum_rate * new_momentum)
    chosen = lax.dynamic_index_in_dim(local_keys[0], fragment[0], 0, keepdims=False)
    synced_keys = (
        keep_share * chosen.astype(jnp.float32) + (1.0 - keep_share) * new_weights
    ).astype(jnp.bfloat16)[None]
    input_grads = put_blocks(
        here, after(grads, synced_keys), near_there, across_there, last_there
    )
    home_kept = after(home[0], (input_grads, synced_keys))
    weight_grads = add_blocks(home_kept, home_one, home_two, home_three, crossed)[None]
    return (input_grads, weight_grads, new_weights, new_momentum, synced_keys)


def solution(mesh):
    placed = (
        P(("island", "fsdp"), None),
        P(("island", "fsdp"), None),
        P("island", None, "fsdp", None),
        P("island", "fsdp", None),
        P("island", "fsdp", None),
        P("fsdp", None),
        P("fsdp", None),
        P("island"),
    )
    return jax.shard_map(
        local,
        mesh=mesh,
        in_specs=placed,
        out_specs=(
            P(("island", "fsdp"), None),
            P("island", "fsdp", None),
            P("fsdp", None),
            P("fsdp", None),
            P("island", "fsdp", None),
        ),
        check_vma=False,
    )
```

time: 204 us -> 101 us (0.50)
  waiting for transfers between devices: 154 us -> 13.8 us
  starting transfers between devices: 0.13 us -> 40.2 us
  Pallas kernels: 0 us -> 35.1 us
  matrix products: 24.3 us -> 0 us
  between operations: 16.2 us -> 1.49 us
  local copies, waits for them, and re-layouts: 2.35 us -> 5.81 us
  other arithmetic: 6.54 us -> 4.25 us
    reduce_scatter x1 -> x0, waiting for transfers between devices: 80.8 us -> none  [local(): lax.psum_scatter(jnp.einsum('td,tk->dk', tokens, key_cotangent, preferred...]
    psum x1 -> x0, waiting for transfers between devices: 72.7 us -> none  [local(): lax.psum(island_delta.astype(jnp.bfloat16), 'island').astype(jnp.float32)]
    ppermute x0 -> x23, starting transfers between devices: none -> 40.2 us  [the longest x5 13 us: to_z(): return lax.ppermute(value, 'fsdp', fsdp_perm(lambda h, x, c: (h + 1, x, c)))]
    pallas_call x0 -> x10, Pallas kernels: none -> 35.1 us  [the longest x2 15.3 us: chip_terms(): pl.pallas_call(body, grid_spec=pltpu.PrefetchScalarGridSpec(num_scalar_pr...]
    dot_general x2 -> x0, matrix products: 24.3 us -> none  [the longest x1 12.5 us: local(): jnp.einsum('tk,dk->td', key_cotangent, lax.all_gather(key_layer, 'fsdp',...]
    ppermute x0 -> x23, waiting for transfers between devices: none -> 13.8 us  [the longest x5 6.19 us: to_z(): return lax.ppermute(value, 'fsdp', fsdp_perm(lambda h, x, c: (h + 1, x, c)))]
    unnamed x4 -> x33, local copies, waits for them, and re-layouts: 0.01 us -> 4.73 us
    convert_element_type x1 -> x0, other arithmetic: 2.3 us -> none  [local(): island_delta.astype(jnp.bfloat16)]
  transfers between devices with their start and end apart: 3 -> 23, of which waited for: 2 -> 9; matrix products, arithmetic and copies ran while one was open for 15% -> 6% of each run, Pallas kernels for 0% -> 33%
where the time goes in v2:
time: 101 us
  starting transfers between devices  40.2 us (40%)
  Pallas kernels  35.1 us (35%)
  waiting for transfers between devices  13.8 us (14%)
  local copies, waits for them, and re-layouts  5.81 us (6%)
  other arithmetic  4.25 us (4%)
  between operations  1.49 us (1%)
    pallas_call x2, Pallas kernels, chip_terms(): pl.pallas_call(body, grid_spec=pltpu.PrefetchScalarGridSpec(num_scalar_pr...  15.3 us
    ppermute x5, starting transfers between devices, to_z(): return lax.ppermute(value, 'fsdp', fsdp_perm(lambda h, x, c: (h + 1, x, c)))  13 us
    ppermute x9, starting transfers between devices, to_x(): lax.ppermute(value, 'fsdp', fsdp_perm(lambda h, x, c: (h, x + step, c)))  12.8 us
    pallas_call x3, Pallas kernels, side_products(): pl.pallas_call(body, grid_spec=pltpu.PrefetchScalarGridSpec(num_scalar_pr...  12.3 us
    ppermute x4, starting transfers between devices, to_island(): return lax.ppermute(value, 'island', pairs)  7.37 us
    ppermute x5, starting transfers between devices, to_core(): return lax.ppermute(value, 'fsdp', fsdp_perm(lambda h, x, c: (h, x, 1 - c)))  7.09 us
    ppermute x5, waiting for transfers between devices, to_z(): return lax.ppermute(value, 'fsdp', fsdp_perm(lambda h, x, c: (h + 1, x, c)))  6.19 us
    ppermute x9, waiting for transfers between devices, to_x(): lax.ppermute(value, 'fsdp', fsdp_perm(lambda h, x, c: (h, x + step, c)))  5.19 us
  transfers between devices with their start and end apart: 23, of which 9 were waited for; matrix products, arithmetic and copies ran while one was open for 6% of the time, Pallas kernels for 33%

profile of v2, /device:TPU:1, one launch (start us, length us, event | category | flops | bytes accessed | tf_op | source)
XLA Modules:
  0.0 100.6 jit_solution(46586191680394278)
XLA Ops:
  6.1 3.7 %collective-permute-start.6 = (bf16[256,1024]{1,0:T(8,128)(2,1)S(1)}, bf16[256,1024]{1,0:T(8,128)(2,1)S(1)}, u32[]{:S(2)}, u32[]{:S(2)}) collective-permute-start(bf16[256,1024]{1,0:T(8,128)(2,1)S(1)} %slice_bitcast_fusion.rest_0_), channel_id=1, source_target_pairs={{0,8},{1,9},{2,10},{3,11},{4,12},{5,13},{6,14},{7,15},{8,0},{9,1},... | collective-permute-start | bytes 1572872 | tf_op jit(solution)/shard_map/ppermute | solution.py:39
  12.5 1.7 %collective-permute-start.8 = (bf16[256,1024]{1,0:T(8,128)(2,1)S(1)}, bf16[256,1024]{1,0:T(8,128)(2,1)}, u32[]{:S(2)}, u32[]{:S(2)}) collective-permute-start(bf16[256,1024]{1,0:T(8,128)(2,1)S(1)} %dequantize.1.refs_0_), channel_id=1, source_target_pairs={{0,16},{16,0},{32,48},{48,32},{64,80},{80,64},{96,112},{112,96},{1... | collective-permute-start | bytes 1572872 | tf_op jit(solution)/shard_map/ppermute | solution.py:48
  14.5 2.8 %collective-permute-start.9 = (bf16[256,1024]{1,0:T(8,128)(2,1)S(1)}, bf16[256,1024]{1,0:T(8,128)(2,1)}, u32[]{:S(2)}, u32[]{:S(2)}) collective-permute-start(bf16[256,1024]{1,0:T(8,128)(2,1)S(1)} %slice_bitcast_fusion.rest_0_), channel_id=1, source_target_pairs={{0,4},{1,5},{2,6},{3,7},{4,0},{5,1},{6,2},{7,3},{8,12},{9,13},{10,... | collective-permute-start | bytes 1572872 | tf_op jit(solution)/shard_map/ppermute | solution.py:35
  17.3 7.6 %chip_terms.2 = (bf16[256,1024]{1,0:T(8,128)(2,1)}, bf16[256,1024]{1,0:T(8,128)(2,1)}, bf16[256,1024]{1,0:T(8,128)(2,1)}, bf16[256,1024]{1,0:T(8,128)(2,1)}) custom-call(s32[1]{0:T(128)} %bitcast.order_ref, bf16[768,4096]{1,0:T(8,128)(2,1)} %tok_ref.3, bf16[768,1024]{1,0:T(8,128)(2,1)} %kc_ref.9, bf16[768,4096]{1,0:T(8,128)(2,1)} %collective-permute-done.their_tok_ref, ...), custom_call_target="tpu_custom_call" | custom-call | flops 966367616 | bytes 3774873 | tf_op jit(solution)/shard_map/chip_terms/pallas_call | solution.py:108
  25.0 3.7 %collective-permute-start.7 = (bf16[256,1024]{1,0:T(8,128)(2,1)}, bf16[256,1024]{1,0:T(8,128)(2,1)S(1)}, u32[]{:S(2)}, u32[]{:S(2)}) collective-permute-start(bf16[256,1024]{1,0:T(8,128)(2,1)} %collective-permute-done.4.rest_2_), channel_id=1, source_target_pairs={{0,8},{1,9},{2,10},{3,11},{4,12},{5,13},{6,14},{7,15},{8,0},{9,1},... | collective-permute-start | bytes 1572872 | tf_op jit(solution)/shard_map/ppermute | solution.py:39
  28.9 2.4 %collective-permute-start.3 = (bf16[256,1024]{1,0:T(8,128)(2,1)}, bf16[256,1024]{1,0:T(8,128)(2,1)S(1)}, u32[]{:S(2)}, u32[]{:S(2)}) collective-permute-start(bf16[256,1024]{1,0:T(8,128)(2,1)} %get-tuple-element.75), channel_id=1, source_target_pairs={{0,6},{1,7},{2,0},{3,1},{4,2},{5,3},{6,4},{7,5},{8,14},{9,15},{10,... | collective-permute-start | bytes 1572872 | tf_op jit(solution)/shard_map/ppermute | solution.py:35
  31.3 7.7 %chip_terms.3 = (bf16[256,1024]{1,0:T(8,128)(2,1)}, bf16[256,1024]{1,0:T(8,128)(2,1)}, bf16[256,1024]{1,0:T(8,128)(2,1)}, bf16[256,1024]{1,0:T(8,128)(2,1)}) custom-call(s32[1]{0:T(128)} %bitcast.order_ref, bf16[768,4096]{1,0:T(8,128)(2,1)} %tok_ref.3, bf16[768,1024]{1,0:T(8,128)(2,1)} %kc_ref.9, bf16[768,4096]{1,0:T(8,128)(2,1)} %collective-permute-done.their_tok_ref, ...), custom_call_target="tpu_custom_call" | custom-call | flops 966367616 | bytes 3774873 | tf_op jit(solution)/shard_map/chip_terms/pallas_call | solution.py:108
  40.3 3.2 %collective-permute-done.7.rest_2_ = bf16[256,1024]{1,0:T(8,128)(2,1)S(1)} collective-permute-done((bf16[256,1024]{1,0:T(8,128)(2,1)}, bf16[256,1024]{1,0:T(8,128)(2,1)S(1)}, u32[]{:S(2)}, u32[]{:S(2)}) %collective-permute-start.7) | collective-permute-done | bytes 524320 | tf_op jit(solution)/shard_map/ppermute | solution.py:39
  43.6 1.6 %collective-permute-start.10 = (bf16[256,1024]{1,0:T(8,128)(2,1)}, bf16[256,1024]{1,0:T(8,128)(2,1)S(1)}, u32[]{:S(2)}, u32[]{:S(2)}) collective-permute-start(bf16[256,1024]{1,0:T(8,128)(2,1)} %get-tuple-element.88), channel_id=1, source_target_pairs={{0,4},{1,5},{2,6},{3,7},{4,0},{5,1},{6,2},{7,3},{8,12},{9,13},{10,... | collective-permute-start | bytes 1572872 | tf_op jit(solution)/shard_map/ppermute | solution.py:35
  45.2 2.6 %collective-permute-start.11 = (bf16[256,1024]{1,0:T(8,128)(2,1)}, bf16[256,1024]{1,0:T(8,128)(2,1)S(1)}, u32[]{:S(2)}, u32[]{:S(2)}) collective-permute-start(bf16[256,1024]{1,0:T(8,128)(2,1)} %collective-permute-done.5.rest_1_), channel_id=1, source_target_pairs={{0,8},{1,9},{2,10},{3,11},{4,12},{5,13},{6,14},{7,15},{8,0},{9,1},... | collective-permute-start | bytes 1572872 | tf_op jit(solution)/shard_map/ppermute | solution.py:39
  50.6 6.3 %side_products.3 = (bf16[768,4096]{1,0:T(8,128)(2,1)}, bf16[4,768,256]{2,1,0:T(8,128)(2,1)S(1)}) custom-call(s32[1]{0:T(128)} %bitcast.order_ref, bf16[768,1024]{1,0:T(8,128)(2,1)S(1)} %copy-done, bf16[768,1024]{1,0:T(8,128)(2,1)S(1)} %copy-done.2, bf16[256,1024]{1,0:T(8,128)(2,1)S(1)} %slice_bitcast_fusion.rest_0_, ...), custom_call_target="tpu_custom_call" | custom-call | flops 966367616 | bytes 2516582 | tf_op jit(solution)/shard_map/side_products/pallas_call | solution.py:161
  58.4 1.8 %collective-permute-done.12 = bf16[256,1024]{1,0:T(8,128)(2,1)} collective-permute-done((bf16[256,1024]{1,0:T(8,128)(2,1)S(1)}, bf16[256,1024]{1,0:T(8,128)(2,1)}, u32[]{:S(2)}, u32[]{:S(2)}) %collective-permute-start.12) | collective-permute-done | bytes 524320 | tf_op jit(solution)/shard_map/ppermute | solution.py:48
  61.0 3.3 %collective-permute-start.17 = (bf16[4,768,256]{2,1,0:T(8,128)(2,1)S(1)}, bf16[4,768,256]{2,1,0:T(8,128)(2,1)S(1)}, u32[]{:S(2)}, u32[]{:S(2)}) collective-permute-start(bf16[4,768,256]{2,1,0:T(8,128)(2,1)S(1)} %get-tuple-element.102), channel_id=1, source_target_pairs={{0,1},{1,0},{2,3},{3,2},{4,5},{5,4},{6,7},{7,6},{8,9},{9,8},{10,11... | collective-permute-start | bytes 4718600 | tf_op jit(solution)/shard_map/ppermute | solution.py:60
  64.7 2.4 %collective-permute-start.15 = (bf16[256,1024]{1,0:T(8,128)(2,1)S(1)}, bf16[256,1024]{1,0:T(8,128)(2,1)S(1)}, u32[]{:S(2)}, u32[]{:S(2)}) collective-permute-start(bf16[256,1024]{1,0:T(8,128)(2,1)S(1)} %copy-done.14), channel_id=1, source_target_pairs={{0,6},{1,7},{2,0},{3,1},{4,2},{5,3},{6,4},{7,5},{8,14},{9,15},{10,... | collective-permute-start | bytes 1572872 | tf_op jit(solution)/shard_map/ppermute | solution.py:35
  67.4 2.9 %collective-permute-start.18 = (bf16[256,1024]{1,0:T(8,128)(2,1)S(1)}, bf16[256,1024]{1,0:T(8,128)(2,1)S(1)}, u32[]{:S(2)}, u32[]{:S(2)}) collective-permute-start(bf16[256,1024]{1,0:T(8,128)(2,1)S(1)} %add_blocks.3), channel_id=1, source_target_pairs={{0,64},{16,80},{32,96},{48,112},{64,0},{80,16},{96,32},{112,48},{1... | collective-permute-start | bytes 1572872 | tf_op jit(solution)/shard_map/ppermute | solution.py:48
  72.3 4.1 %side_products.4 = (bf16[768,4096]{1,0:T(8,128)(2,1)}, bf16[3,768,256]{2,1,0:T(8,128)(2,1)}) custom-call(s32[1]{0:T(128)} %bitcast.order_ref, bf16[768,1024]{1,0:T(8,128)(2,1)S(1)} %copy-done, bf16[768,1024]{1,0:T(8,128)(2,1)S(1)} %copy-done.2, bf16[256,1024]{1,0:T(8,128)(2,1)S(1)} %collective-permute-done.6.rest_0_, ...), custom_call_target="tpu_custom_call", output_to_operand_aliasing={{0}: (6, {})} | custom-call | flops 724775744 | bytes 1887436 | tf_op jit(solution)/shard_map/side_products/pallas_call | solution.py:161
  76.4 2.7 %collective-permute-done.14.refs_1_ = bf16[256,1024]{1,0:T(8,128)(2,1)S(1)} collective-permute-done((bf16[256,1024]{1,0:T(8,128)(2,1)S(1)}, bf16[256,1024]{1,0:T(8,128)(2,1)S(1)}, u32[]{:S(2)}, u32[]{:S(2)}) %collective-permute-start.14) | collective-permute-done | bytes 524320 | tf_op jit(solution)/shard_map/ppermute | solution.py:35
  79.9 1.7 %collective-permute-done.16.rest_0_ = bf16[256,1024]{1,0:T(8,128)(2,1)S(1)} collective-permute-done((bf16[256,1024]{1,0:T(8,128)(2,1)}, bf16[256,1024]{1,0:T(8,128)(2,1)S(1)}, u32[]{:S(2)}, u32[]{:S(2)}) %collective-permute-start.16) | collective-permute-done | bytes 524320 | tf_op jit(solution)/shard_map/ppermute | solution.py:39
  83.5 2.6 %collective-permute-start.22 = (bf16[256,1024]{1,0:T(8,128)(2,1)}, bf16[256,1024]{1,0:T(8,128)(2,1)}, u32[]{:S(2)}, u32[]{:S(2)}) collective-permute-start(bf16[256,1024]{1,0:T(8,128)(2,1)} %add_blocks.4), channel_id=1, source_target_pairs={{0,8},{1,9},{2,10},{3,11},{4,12},{5,13},{6,14},{7,15},{8,0},{9,1},... | collective-permute-start | bytes 1572872 | tf_op jit(solution)/shard_map/ppermute | solution.py:39
  86.1 1.9 %side_products.5 = (bf16[768,4096]{1,0:T(8,128)(2,1)}, bf16[1,768,256]{2,1,0:T(8,128)(2,1)}) custom-call(s32[1]{0:T(128)} %bitcast.order_ref, bf16[768,1024]{1,0:T(8,128)(2,1)S(1)} %copy-done, bf16[768,1024]{1,0:T(8,128)(2,1)S(1)} %copy-done.2, bf16[256,1024]{1,0:T(8,128)(2,1)S(1)} %collective-permute-done.16.rest_0_, ...), custom_call_target="tpu_custom_call", output_to_operand_aliasing={{0}: (4, {})} | custom-call | flops 241591904 | bytes 629145 | tf_op jit(solution)/shard_map/side_products/pallas_call | solution.py:161
  89.3 4.3 %fusion.2 = (bf16[1,256,1024]{2,1,0:T(8,128)(2,1)}, f32[256,1024]{1,0:T(8,128)}, f32[256,1024]{1,0:T(8,128)}) fusion(bf16[1,4,256,1024]{3,2,1,0:T(8,128)(2,1)} %param.10, s32[]{:T(128)S(6)} %select_n.4, f32[256,1024]{1,0:T(8,128)} %param.13, bf16[256,1024]{1,0:T(8,128)(2,1)} %copy-done.13, bf16[256,1024]{1,0:T(8,128)(2,1)} %copy-done.12, ...), kind=kLoop, calls=%fused_computation.6 | loop fusion | flops 4718592 | bytes 7340036 | tf_op jit(solution)/shard_map/broadcast_in_dim | solution.py:337
  93.5 2.8 %put_blocks.1 = bf16[768,4096]{1,0:T(8,128)(2,1)} custom-call(s32[1]{0:T(128)} %bitcast.order_ref, bf16[4,768,256]{2,1,0:T(8,128)(2,1)S(1)} %collective-permute-done.17.rest_0_, bf16[3,768,256]{2,1,0:T(8,128)(2,1)S(1)} %collective-permute-done.19.rest_1_, bf16[1,768,256]{2,1,0:T(8,128)(2,1)} %collective-permute-done.20.rest_2_, ...), custom_call_target="tpu_custom_call", output_to_operand_aliasing={{}: (4, {})} | custom-call | bytes 1887436 | tf_op jit(solution)/shard_map/put_blocks/pallas_call | solution.py:206
  96.4 2.1 %collective-permute-done.21.refs_2_ = bf16[256,1024]{1,0:T(8,128)(2,1)} collective-permute-done((bf16[256,1024]{1,0:T(8,128)(2,1)}, bf16[256,1024]{1,0:T(8,128)(2,1)}, u32[]{:S(2)}, u32[]{:S(2)}) %collective-permute-start.21) | collective-permute-done | bytes 524320 | tf_op jit(solution)/shard_map/ppermute | solution.py:35
  98.5 2.1 %add_blocks.5 = bf16[256,1024]{1,0:T(8,128)(2,1)} custom-call(bf16[256,1024]{1,0:T(8,128)(2,1)S(1)} %copy-done.7, bf16[256,1024]{1,0:T(8,128)(2,1)S(1)} %copy-done.9, bf16[256,1024]{1,0:T(8,128)(2,1)} %collective-permute-done.21.refs_2_, bf16[256,1024]{1,0:T(8,128)(2,1)S(1)} %copy-done.11, bf16[256,1024]{1,0:T(8,128)(2,1)} %collective-permute-done.22.refs_4_), custom_call_target="tpu_custom_call" | custom-call | flops 393216 | bytes 943718 | tf_op jit(solution)/shard_map/add_blocks/pallas_call | solution.py:258
  (67 shorter events, 21.0 us)
Async XLA Ops:
  0.6 13.9 %collective-permute-start = (bf16[768,4096]{1,0:T(8,128)(2,1)}, bf16[768,4096]{1,0:T(8,128)(2,1)}, u32[]{:S(2)}, u32[]{:S(2)}) collective-permute-start(bf16[768,4096]{1,0:T(8,128)(2,1)} %tok_ref.3), channel_id=1, source_target_pairs={{0,1},{1,0},{2,3},{3,2},{4,5},{5,4},{6,7},{7,6},{8,9},{9,8},{10,11... | collective-permute-start | bytes 18874376 | tf_op jit(solution)/shard_map/ppermute | solution.py:60
  2.1 10.4 %collective-permute-start.1 = (bf16[768,1024]{1,0:T(8,128)(2,1)}, bf16[768,1024]{1,0:T(8,128)(2,1)S(1)}, u32[]{:S(2)}, u32[]{:S(2)}) collective-permute-start(bf16[768,1024]{1,0:T(8,128)(2,1)} %kc_ref.9), channel_id=1, source_target_pairs={{0,1},{1,0},{2,3},{3,2},{4,5},{5,4},{6,7},{7,6},{8,9},{9,8},{10,11... | collective-permute-start | bytes 4718600 | tf_op jit(solution)/shard_map/ppermute | solution.py:60
  3.3 21.6 %collective-permute-start.4 = (bf16[256,1024]{1,0:T(8,128)(2,1)S(1)}, bf16[256,1024]{1,0:T(8,128)(2,1)}, u32[]{:S(2)}, u32[]{:S(2)}) collective-permute-start(bf16[256,1024]{1,0:T(8,128)(2,1)S(1)} %slice_bitcast_fusion.rest_0_), channel_id=1, source_target_pairs={{0,2},{1,3},{2,4},{3,5},{4,6},{5,7},{6,0},{7,1},{8,10},{9,11},{10,... | collective-permute-start | bytes 1572872 | tf_op jit(solution)/shard_map/ppermute | solution.py:35
  4.7 20.3 %collective-permute-start.5 = (bf16[256,1024]{1,0:T(8,128)(2,1)S(1)}, bf16[256,1024]{1,0:T(8,128)(2,1)}, u32[]{:S(2)}, u32[]{:S(2)}) collective-permute-start(bf16[256,1024]{1,0:T(8,128)(2,1)S(1)} %slice_bitcast_fusion.rest_0_), channel_id=1, source_target_pairs={{0,6},{1,7},{2,0},{3,1},{4,2},{5,3},{6,4},{7,5},{8,14},{9,15},{10,... | collective-permute-start | bytes 1572872 | tf_op jit(solution)/shard_map/ppermute | solution.py:35
  6.1 18.9 %collective-permute-start.6 = (bf16[256,1024]{1,0:T(8,128)(2,1)S(1)}, bf16[256,1024]{1,0:T(8,128)(2,1)S(1)}, u32[]{:S(2)}, u32[]{:S(2)}) collective-permute-start(bf16[256,1024]{1,0:T(8,128)(2,1)S(1)} %slice_bitcast_fusion.rest_0_), channel_id=1, source_target_pairs={{0,8},{1,9},{2,10},{3,11},{4,12},{5,13},{6,14},{7,15},{8,0},{9,1},... | collective-permute-start | bytes 1572872 | tf_op jit(solution)/shard_map/ppermute | solution.py:39
  12.5 26.5 %collective-permute-start.8 = (bf16[256,1024]{1,0:T(8,128)(2,1)S(1)}, bf16[256,1024]{1,0:T(8,128)(2,1)}, u32[]{:S(2)}, u32[]{:S(2)}) collective-permute-start(bf16[256,1024]{1,0:T(8,128)(2,1)S(1)} %dequantize.1.refs_0_), channel_id=1, source_target_pairs={{0,16},{16,0},{32,48},{48,32},{64,80},{80,64},{96,112},{112,96},{1... | collective-permute-start | bytes 1572872 | tf_op jit(solution)/shard_map/ppermute | solution.py:48
  14.5 25.8 %collective-permute-start.9 = (bf16[256,1024]{1,0:T(8,128)(2,1)S(1)}, bf16[256,1024]{1,0:T(8,128)(2,1)}, u32[]{:S(2)}, u32[]{:S(2)}) collective-permute-start(bf16[256,1024]{1,0:T(8,128)(2,1)S(1)} %slice_bitcast_fusion.rest_0_), channel_id=1, source_target_pairs={{0,4},{1,5},{2,6},{3,7},{4,0},{5,1},{6,2},{7,3},{8,12},{9,13},{10,... | collective-permute-start | bytes 1572872 | tf_op jit(solution)/shard_map/ppermute | solution.py:35
  25.0 18.6 %collective-permute-start.7 = (bf16[256,1024]{1,0:T(8,128)(2,1)}, bf16[256,1024]{1,0:T(8,128)(2,1)S(1)}, u32[]{:S(2)}, u32[]{:S(2)}) collective-permute-start(bf16[256,1024]{1,0:T(8,128)(2,1)} %collective-permute-done.4.rest_2_), channel_id=1, source_target_pairs={{0,8},{1,9},{2,10},{3,11},{4,12},{5,13},{6,14},{7,15},{8,0},{9,1},... | collective-permute-start | bytes 1572872 | tf_op jit(solution)/shard_map/ppermute | solution.py:39
  28.6 14.9 %collective-permute-start.2 = (bf16[256,1024]{1,0:T(8,128)(2,1)}, bf16[256,1024]{1,0:T(8,128)(2,1)S(1)}, u32[]{:S(2)}, u32[]{:S(2)}) collective-permute-start(bf16[256,1024]{1,0:T(8,128)(2,1)} %get-tuple-element.73), channel_id=1, source_target_pairs={{0,2},{1,3},{2,4},{3,5},{4,6},{5,7},{6,0},{7,1},{8,10},{9,11},{10,... | collective-permute-start | bytes 1572872 | tf_op jit(solution)/shard_map/ppermute | solution.py:35
  28.9 14.6 %collective-permute-start.3 = (bf16[256,1024]{1,0:T(8,128)(2,1)}, bf16[256,1024]{1,0:T(8,128)(2,1)S(1)}, u32[]{:S(2)}, u32[]{:S(2)}) collective-permute-start(bf16[256,1024]{1,0:T(8,128)(2,1)} %get-tuple-element.75), channel_id=1, source_target_pairs={{0,6},{1,7},{2,0},{3,1},{4,2},{5,3},{6,4},{7,5},{8,14},{9,15},{10,... | collective-permute-start | bytes 1572872 | tf_op jit(solution)/shard_map/ppermute | solution.py:35
  43.5 26.7 %copy-start.4 = (bf16[256,1024]{1,0:T(8,128)(2,1)S(1)}, bf16[256,1024]{1,0:T(8,128)(2,1)}, u32[]{:S(2)}) copy-start(bf16[256,1024]{1,0:T(8,128)(2,1)} %get-tuple-element.104.refs_0_) | copy-start | bytes 1572868
  43.6 13.6 %collective-permute-start.10 = (bf16[256,1024]{1,0:T(8,128)(2,1)}, bf16[256,1024]{1,0:T(8,128)(2,1)S(1)}, u32[]{:S(2)}, u32[]{:S(2)}) collective-permute-start(bf16[256,1024]{1,0:T(8,128)(2,1)} %get-tuple-element.88), channel_id=1, source_target_pairs={{0,4},{1,5},{2,6},{3,7},{4,0},{5,1},{6,2},{7,3},{8,12},{9,13},{10,... | collective-permute-start | bytes 1572872 | tf_op jit(solution)/shard_map/ppermute | solution.py:35
  45.2 13.3 %collective-permute-start.11 = (bf16[256,1024]{1,0:T(8,128)(2,1)}, bf16[256,1024]{1,0:T(8,128)(2,1)S(1)}, u32[]{:S(2)}, u32[]{:S(2)}) collective-permute-start(bf16[256,1024]{1,0:T(8,128)(2,1)} %collective-permute-done.5.rest_1_), channel_id=1, source_target_pairs={{0,8},{1,9},{2,10},{3,11},{4,12},{5,13},{6,14},{7,15},{8,0},{9,1},... | collective-permute-start | bytes 1572872 | tf_op jit(solution)/shard_map/ppermute | solution.py:39
  47.8 12.4 %collective-permute-start.12 = (bf16[256,1024]{1,0:T(8,128)(2,1)S(1)}, bf16[256,1024]{1,0:T(8,128)(2,1)}, u32[]{:S(2)}, u32[]{:S(2)}) collective-permute-start(bf16[256,1024]{1,0:T(8,128)(2,1)S(1)} %add_blocks.3), channel_id=1, source_target_pairs={{0,32},{16,48},{32,64},{48,80},{64,96},{80,112},{96,0},{112,16},{1... | collective-permute-start | bytes 1572872 | tf_op jit(solution)/shard_map/ppermute | solution.py:48
  49.1 11.1 %collective-permute-start.13 = (bf16[256,1024]{1,0:T(8,128)(2,1)S(1)}, bf16[256,1024]{1,0:T(8,128)(2,1)S(1)}, u32[]{:S(2)}, u32[]{:S(2)}) collective-permute-start(bf16[256,1024]{1,0:T(8,128)(2,1)S(1)} %add_blocks.3), channel_id=1, source_target_pairs={{0,96},{16,112},{32,0},{48,16},{64,32},{80,48},{96,64},{112,80},{1... | collective-permute-start | bytes 1572872 | tf_op jit(solution)/shard_map/ppermute | solution.py:48
  61.0 20.6 %collective-permute-start.17 = (bf16[4,768,256]{2,1,0:T(8,128)(2,1)S(1)}, bf16[4,768,256]{2,1,0:T(8,128)(2,1)S(1)}, u32[]{:S(2)}, u32[]{:S(2)}) collective-permute-start(bf16[4,768,256]{2,1,0:T(8,128)(2,1)S(1)} %get-tuple-element.102), channel_id=1, source_target_pairs={{0,1},{1,0},{2,3},{3,2},{4,5},{5,4},{6,7},{7,6},{8,9},{9,8},{10,11... | collective-permute-start | bytes 4718600 | tf_op jit(solution)/shard_map/ppermute | solution.py:60
  64.3 14.8 %collective-permute-start.14 = (bf16[256,1024]{1,0:T(8,128)(2,1)S(1)}, bf16[256,1024]{1,0:T(8,128)(2,1)S(1)}, u32[]{:S(2)}, u32[]{:S(2)}) collective-permute-start(bf16[256,1024]{1,0:T(8,128)(2,1)S(1)} %copy-done.15), channel_id=1, source_target_pairs={{0,2},{1,3},{2,4},{3,5},{4,6},{5,7},{6,0},{7,1},{8,10},{9,11},{10,... | collective-permute-start | bytes 1572872 | tf_op jit(solution)/shard_map/ppermute | solution.py:35
  64.7 15.2 %collective-permute-start.15 = (bf16[256,1024]{1,0:T(8,128)(2,1)S(1)}, bf16[256,1024]{1,0:T(8,128)(2,1)S(1)}, u32[]{:S(2)}, u32[]{:S(2)}) collective-permute-start(bf16[256,1024]{1,0:T(8,128)(2,1)S(1)} %copy-done.14), channel_id=1, source_target_pairs={{0,6},{1,7},{2,0},{3,1},{4,2},{5,3},{6,4},{7,5},{8,14},{9,15},{10,... | collective-permute-start | bytes 1572872 | tf_op jit(solution)/shard_map/ppermute | solution.py:35
  67.0 14.6 %collective-permute-start.16 = (bf16[256,1024]{1,0:T(8,128)(2,1)}, bf16[256,1024]{1,0:T(8,128)(2,1)S(1)}, u32[]{:S(2)}, u32[]{:S(2)}) collective-permute-start(bf16[256,1024]{1,0:T(8,128)(2,1)} %collective-permute-done.9.rest_3_), channel_id=1, source_target_pairs={{0,8},{1,9},{2,10},{3,11},{4,12},{5,13},{6,14},{7,15},{8,0},{9,1},... | collective-permute-start | bytes 1572872 | tf_op jit(solution)/shard_map/ppermute | solution.py:39
  67.4 14.3 %collective-permute-start.18 = (bf16[256,1024]{1,0:T(8,128)(2,1)S(1)}, bf16[256,1024]{1,0:T(8,128)(2,1)S(1)}, u32[]{:S(2)}, u32[]{:S(2)}) collective-permute-start(bf16[256,1024]{1,0:T(8,128)(2,1)S(1)} %add_blocks.3), channel_id=1, source_target_pairs={{0,64},{16,80},{32,96},{48,112},{64,0},{80,16},{96,32},{112,48},{1... | collective-permute-start | bytes 1572872 | tf_op jit(solution)/shard_map/ppermute | solution.py:48
  81.7 11.9 %collective-permute-start.19 = (bf16[3,768,256]{2,1,0:T(8,128)(2,1)}, bf16[3,768,256]{2,1,0:T(8,128)(2,1)S(1)}, u32[]{:S(2)}, u32[]{:S(2)}) collective-permute-start(bf16[3,768,256]{2,1,0:T(8,128)(2,1)} %get-tuple-element.119), channel_id=1, source_target_pairs={{0,1},{1,0},{2,3},{3,2},{4,5},{5,4},{6,7},{7,6},{8,9},{9,8},{10,11... | collective-permute-start | bytes 3538952 | tf_op jit(solution)/shard_map/ppermute | solution.py:60
  83.2 15.3 %collective-permute-start.21 = (bf16[256,1024]{1,0:T(8,128)(2,1)}, bf16[256,1024]{1,0:T(8,128)(2,1)}, u32[]{:S(2)}, u32[]{:S(2)}) collective-permute-start(bf16[256,1024]{1,0:T(8,128)(2,1)} %get-tuple-element.132), channel_id=1, source_target_pairs={{0,4},{1,5},{2,6},{3,7},{4,0},{5,1},{6,2},{7,3},{8,12},{9,13},{10,... | collective-permute-start | bytes 1572872 | tf_op jit(solution)/shard_map/ppermute | solution.py:35
  83.5 15.1 %collective-permute-start.22 = (bf16[256,1024]{1,0:T(8,128)(2,1)}, bf16[256,1024]{1,0:T(8,128)(2,1)}, u32[]{:S(2)}, u32[]{:S(2)}) collective-permute-start(bf16[256,1024]{1,0:T(8,128)(2,1)} %add_blocks.4), channel_id=1, source_target_pairs={{0,8},{1,9},{2,10},{3,11},{4,12},{5,13},{6,14},{7,15},{8,0},{9,1},... | collective-permute-start | bytes 1572872 | tf_op jit(solution)/shard_map/ppermute | solution.py:39
  88.0 5.6 %collective-permute-start.20 = (bf16[1,768,256]{2,1,0:T(8,128)(2,1)}, bf16[1,768,256]{2,1,0:T(8,128)(2,1)}, u32[]{:S(2)}, u32[]{:S(2)}) collective-permute-start(bf16[1,768,256]{2,1,0:T(8,128)(2,1)} %get-tuple-element.122), channel_id=1, source_target_pairs={{0,1},{1,0},{2,3},{3,2},{4,5},{5,4},{6,7},{7,6},{8,9},{9,8},{10,11... | collective-permute-start | bytes 1179656 | tf_op jit(solution)/shard_map/ppermute | solution.py:60
  (15 other events, 124.2 us)

commit v3 on v2

--- a/solution.py
+++ b/solution.py
@@ -11,6 +11,7 @@
 
 ISLANDS = 8
 BLK = 256
+HALF = BLK // 2
 MIB = 1 << 20
 TERM_MIB = 58
 INPUT_MIB = 24
@@ -48,8 +49,9 @@
     return lax.ppermute(value, "island", pairs)
 
 
-def to_y(value, step):
-    return to_island(value, lambda y, side: (y + step, side))
+def over_y(copies):
+    groups = [[y * 2 + side for y in range(4)] for side in range(2)]
+    return lax.all_to_all(copies, "island", 0, 0, axis_index_groups=groups, tiled=True)
 
 
 def to_side(value):
@@ -84,9 +86,19 @@
 
 def chip_terms(order, side, tokens, kc, their_tokens, their_kc):
     rows, width = kc.shape
+    pieces = [(0, 0, BLK), (1, 0, BLK), (2, 0, HALF), (2, HALF, HALF), (3, 0, BLK)]
+    count = len(pieces)
 
     def body(order_ref, tok_ref, kc_ref, their_tok_ref, their_kc_ref, *rest):
-        outs, held, sems = rest[:4], rest[4], rest[5]
+        outs, held, sems = rest[:count], rest[count], rest[count + 1]
+
+        def copies(block):
+            return [
+                pltpu.make_async_copy(held.at[k, pl.ds(start, size)], outs[n], sems.at[n])
+                for n, (k, start, size) in enumerate(pieces)
+                if block is None or k == block
+            ]
+
         j = pl.program_id(0)
         total = term(tok_ref[...], kc_ref[...])
         total += term(their_tok_ref[...], their_kc_ref[...])
@@ -96,12 +108,13 @@
             @pl.when(j == k)
             def _():
                 held[k] = total
-                pltpu.make_async_copy(held.at[k], outs[k], sems.at[k]).start()
+                for copy in copies(k):
+                    copy.start()
 
         @pl.when(j == 3)
         def _():
-            for k in range(4):
-                pltpu.make_async_copy(held.at[k], outs[k], sems.at[k]).wait()
+            for copy in copies(None):
+                copy.wait()
 
     whole = pl.BlockSpec((rows, width), lambda j, order: (0, 0))
     columns = pl.BlockSpec((rows, BLK), lambda j, order: (0, block_at(order[0], side, j)))
@@ -111,13 +124,13 @@
             num_scalar_prefetch=1,
             grid=(4,),
             in_specs=[columns, whole, columns, whole],
-            out_specs=[pl.BlockSpec(memory_space=pl.ANY)] * 4,
+            out_specs=[pl.BlockSpec(memory_space=pl.ANY)] * count,
             scratch_shapes=[
                 pltpu.VMEM((4, BLK, width), jnp.bfloat16),
-                pltpu.SemaphoreType.DMA((4,)),
+                pltpu.SemaphoreType.DMA((count,)),
             ],
         ),
-        out_shape=[jax.ShapeDtypeStruct((BLK, width), jnp.bfloat16)] * 4,
+        out_shape=[jax.ShapeDtypeStruct((size, width), jnp.bfloat16) for _, _, size in pieces],
         compiler_params=params(TERM_MIB),
         cost_estimate=cost(2 * 8 * rows * BLK * width, 12 * MIB),
         name="chip_terms",
@@ -267,6 +280,66 @@
     )(*blocks)
 
 
+def plain_kernel(body, shapes, name, *operands):
+    return pl.pallas_call(
+        body,
+        out_shape=[jax.ShapeDtypeStruct(shape, jnp.bfloat16) for shape in shapes],
+        compiler_params=params(INPUT_MIB),
+        cost_estimate=cost(0, 6 * MIB),
+        name=name,
+    )(*operands)
+
+
+def rounded_sum(*parts):
+    total = parts[0].astype(jnp.float32)
+    for part in parts[1:]:
+        total = total + part.astype(jnp.float32)
+    return total.astype(jnp.bfloat16)
+
+
+def pair_copies(own, other):
+    rows, width = own.shape
+
+    def body(own_ref, other_ref, out_ref):
+        total = rounded_sum(own_ref[...], other_ref[...])
+        for k in range(4):
+            out_ref[k] = total
+
+    return plain_kernel(body, [(4, rows, width)], "pair_copies", own, other)[0]
+
+
+def relay_away(one, three, from_left, from_right, low, high):
+    width = one.shape[1]
+
+    def body(one_ref, three_ref, left_ref, right_ref, low_ref, high_ref, plus_ref, minus_ref):
+        plus_ref[:HALF] = rounded_sum(one_ref[:HALF], left_ref[...])
+        plus_ref[HALF:BLK] = one_ref[HALF:]
+        plus_ref[BLK:] = low_ref[...]
+        minus_ref[:HALF] = three_ref[:HALF]
+        minus_ref[HALF:BLK] = rounded_sum(three_ref[HALF:], right_ref[...])
+        minus_ref[BLK:] = high_ref[...]
+
+    shapes = [(BLK + HALF, width)] * 2
+    return plain_kernel(
+        body, shapes, "relay_away", one, three, from_left, from_right, low, high
+    )
+
+
+def relay_home(kept, from_left, from_right, one, three):
+    width = kept.shape[1]
+
+    def body(kept_ref, left_ref, right_ref, one_ref, three_ref, sum_ref, plus_ref, minus_ref):
+        sum_ref[...] = rounded_sum(kept_ref[...], left_ref[:BLK], right_ref[:BLK])
+        plus_ref[:HALF] = rounded_sum(one_ref[:HALF], left_ref[BLK:])
+        plus_ref[HALF:] = one_ref[HALF:]
+        minus_ref[:HALF] = three_ref[:HALF]
+        minus_ref[HALF:] = rounded_sum(three_ref[HALF:], right_ref[BLK:])
+
+    return plain_kernel(
+        body, [(BLK, width)] * 3, "relay_home", kept, from_left, from_right, one, three
+    )
+
+
 def local(
     tokens,
     key_cotangent,
@@ -293,55 +366,48 @@
     away = chip_terms(here, 1, tokens, key_cotangent, their_tokens, after(their_kc, delta))
     left, right, peer, delta = after((left, right, peer, delta), away[0])
 
-    away_one = to_x(away[1], 1)
-    away_three = to_x(away[3], -1)
+    low, high = after((away[2], away[3]), (left, right, peer))
+    from_left = to_x(low, 1)
+    from_right = to_x(high, -1)
     peer_left = to_z(left)
     home = chip_terms(here, 0, tokens, key_cotangent, their_tokens, after(their_kc, (peer, right)))
-    pair = add_blocks(after(delta, home[0]), other_delta)
-    away, away_one, away_three, peer_left, pair, home, far, own, right = phase(
-        away, away_one, away_three, peer_left, pair, home, far, own, right
-    )
-
-    away_two = to_x(away[2], 2)
-    peer_right = to_z(right)
-    pair_next = to_y(pair, 1)
-    pair_last = to_y(pair, -1)
+    peer_right = to_z(after(right, (home[0], peer_left)))
+    from_left, from_right, away, home, far, own, other_delta = phase(
+        from_left, from_right, away, home, far, own, other_delta
+    )
+    plus, minus = relay_away(away[1], away[4], from_left, from_right, home[2], home[3])
+
+    away_left = to_x(plus, 1)
+    away_right = to_x(minus, -1)
+    peer_far = to_z(after(far, peer_left))
+    pairs = over_y(pair_copies(after(delta, plus), other_delta))
     near = [own, right, left, far]
-    grads, near_theirs = side_products(here, 0, 0, key_cotangent, their_kc, near, None)
-    away, away_two, peer_right, pair, pair_next, pair_last, grads, near_theirs, home, far = phase(
-        away, away_two, peer_right, pair, pair_next, pair_last, grads, near_theirs, home, far
-    )
-
-    home_one = to_x(home[1], 1)
-    home_three = to_x(home[3], -1)
-    peer_far = to_z(far)
-    near_there = to_core(near_theirs)
-    pair_far = to_y(pair, 2)
-    away_sum = add_blocks(away[0], away_one, away_two, away_three)
-    across = after([peer, peer_right, peer_left], away_sum)
+    grads, near_theirs = side_products(
+        here, 0, 0, key_cotangent, after(their_kc, plus), near, None
+    )
+    away_left, away_right, peer_right, grads, near_theirs = phase(
+        away_left, away_right, peer_right, grads, near_theirs
+    )
+
+    away_sum, plus, minus = relay_home(away[0], away_left, away_right, home[1], home[4])
+    home_left = to_x(plus, 1)
+    home_right = to_x(minus, -1)
+    crossed = to_z(away_sum)
+    near_there = to_core(after(near_theirs, peer_far))
+    across = after([peer, peer_right, peer_left, peer_far], away_sum)
     grads, across_theirs = side_products(here, 1, 0, key_cotangent, their_kc, across, grads)
-    home_one, home_three, peer_far, near_there, pair_far, away_sum, grads, across_theirs, home = phase(
-        home_one, home_three, peer_far, near_there, pair_far, away_sum, grads, across_theirs, home
-    )
-
-    home_two = to_x(home[2], 2)
-    crossed = to_z(away_sum)
-    across_there = to_core(across_theirs)
-    grads, last_theirs = side_products(here, 1, 3, key_cotangent, their_kc, [peer_far], grads)
-    last_there = to_core(last_theirs)
-    pairs = (after(pair, grads), pair_next, pair_last, pair_far)
-    mean_delta = sum(part.astype(jnp.float32) for part in pairs) / ISLANDS
+    across_there = to_core(after(across_theirs, (home_left, home_right, crossed)))
+    pairs = after(pairs, grads)
+    mean_delta = jnp.sum(pairs.astype(jnp.float32), axis=0) / ISLANDS
     new_momentum = momentum_rate * outer_momentum + mean_delta
     new_weights = outer_weights - outer_rate * (mean_delta + momentum_rate * new_momentum)
     chosen = lax.dynamic_index_in_dim(local_keys[0], fragment[0], 0, keepdims=False)
     synced_keys = (
         keep_share * chosen.astype(jnp.float32) + (1.0 - keep_share) * new_weights
     ).astype(jnp.bfloat16)[None]
-    input_grads = put_blocks(
-        here, after(grads, synced_keys), near_there, across_there, last_there
-    )
-    home_kept = after(home[0], (input_grads, synced_keys))
-    weight_grads = add_blocks(home_kept, home_one, home_two, home_three, crossed)[None]
+    input_grads = put_blocks(here, after(grads, synced_keys), near_there, across_there)
+    home_kept = after(home[0], input_grads)
+    weight_grads = add_blocks(home_kept, home_left, home_right, crossed)[None]
     return (input_grads, weight_grads, new_weights, new_momentum, synced_keys)
 
 

time: 101 us -> 95.9 us (0.950)
  waiting for transfers between devices: 13.8 us -> 1.13 us
  local copies, waits for them, and re-layouts: 5.81 us -> 10.7 us
  Pallas kernels: 35.1 us -> 36.9 us
    ppermute x5, waiting for transfers between devices: 6.19 us -> 0.47 us  [to_z(): return lax.ppermute(value, 'fsdp', fsdp_perm(lambda h, x, c: (h + 1, x, c)))]
    ppermute x4 -> x1, starting transfers between devices: 7.37 us -> 1.72 us  [to_island(): return lax.ppermute(value, 'island', pairs)]
    ppermute x9, waiting for transfers between devices: 5.19 us -> 0.02 us  [to_x(): lax.ppermute(value, 'fsdp', fsdp_perm(lambda h, x, c: (h, x + step, c)))]
    unnamed x33 -> x55, local copies, waits for them, and re-layouts: 4.73 us -> 9.62 us
    all_to_all x0 -> x1, starting transfers between devices: none -> 4.71 us  [over_y(): lax.all_to_all(copies, 'island', 0, 0, axis_index_groups=groups, tiled=True)]
    pallas_call x0 -> x3, Pallas kernels: none -> 4.21 us  [plain_kernel(): pl.pallas_call(body, out_shape=[jax.ShapeDtypeStruct(shape, jnp.bfloat16)...]
    pallas_call x3 -> x1, Pallas kernels: 4.31 us -> 1.01 us  [add_blocks(): pl.pallas_call(body, grid=(2,), in_specs=[spec] * len(blocks), out_specs=...]
    reduce_sum x0 -> x1, other arithmetic: none -> 2.19 us  [local(): mean_delta = jnp.sum(pairs.astype(jnp.float32), axis=0) / ISLANDS]
  transfers between devices with their start and end apart: 23 -> 20, of which waited for: 9 -> 3; matrix products, arithmetic and copies ran while one was open for 6% -> 7% of each run, Pallas kernels for 33% -> 34%
where the time goes in v3:
time: 95.9 us; the launch traced here: 95.2 us
  starting transfers between devices  39.7 us (41%)
  Pallas kernels  36.9 us (38%)
  local copies, waits for them, and re-layouts  10.7 us (11%)
  other arithmetic  5.1 us (5%)
  between operations  1.65 us (2%)
  waiting for transfers between devices  1.13 us (1%)
    pallas_call x2, Pallas kernels, chip_terms(): pl.pallas_call(body, grid_spec=pltpu.PrefetchScalarGridSpec(num_scalar_pr...  15.1 us
    ppermute x9, starting transfers between devices, to_x(): lax.ppermute(value, 'fsdp', fsdp_perm(lambda h, x, c: (h, x + step, c)))  13.7 us
    pallas_call x2, Pallas kernels, side_products(): pl.pallas_call(body, grid_spec=pltpu.PrefetchScalarGridSpec(num_scalar_pr...  12.9 us
    ppermute x5, starting transfers between devices, to_z(): return lax.ppermute(value, 'fsdp', fsdp_perm(lambda h, x, c: (h + 1, x, c)))  12.1 us
    unnamed x55, local copies, waits for them, and re-layouts  9.62 us
    ppermute x4, starting transfers between devices, to_core(): return lax.ppermute(value, 'fsdp', fsdp_perm(lambda h, x, c: (h, x, 1 - c)))  7.45 us
    all_to_all x1, starting transfers between devices, over_y(): lax.all_to_all(copies, 'island', 0, 0, axis_index_groups=groups, tiled=True)  4.71 us
    pallas_call x3, Pallas kernels, plain_kernel(): pl.pallas_call(body, out_shape=[jax.ShapeDtypeStruct(shape, jnp.bfloat16)...  4.21 us
  transfers between devices with their start and end apart: 20, of which 3 were waited for; matrix products, arithmetic and copies ran while one was open for 7% of the time, Pallas kernels for 34%

profile of v3, /device:TPU:1, one launch (start us, length us, event | category | flops | bytes accessed | tf_op | source)
XLA Modules:
  0.0 95.2 jit_solution(3734325522324535212)
XLA Ops:
  0.6 1.5 %collective-permute-start = (bf16[768,4096]{1,0:T(8,128)(2,1)}, bf16[768,4096]{1,0:T(8,128)(2,1)}, u32[]{:S(2)}, u32[]{:S(2)}) collective-permute-start(bf16[768,4096]{1,0:T(8,128)(2,1)} %tok_ref.3), channel_id=1, source_target_pairs={{0,1},{1,0},{2,3},{3,2},{4,5},{5,4},{6,7},{7,6},{8,9},{9,8},{10,11... | collective-permute-start | bytes 18874376 | tf_op jit(solution)/shard_map/ppermute | solution.py:62
  3.3 1.4 %collective-permute-start.2 = (bf16[256,1024]{1,0:T(8,128)(2,1)S(1)}, bf16[256,1024]{1,0:T(8,128)(2,1)}, u32[]{:S(2)}, u32[]{:S(2)}) collective-permute-start(bf16[256,1024]{1,0:T(8,128)(2,1)S(1)} %slice_bitcast_fusion.rest_0_), channel_id=1, source_target_pairs={{0,2},{1,3},{2,4},{3,5},{4,6},{5,7},{6,0},{7,1},{8,10},{9,11},{10,... | collective-permute-start | bytes 1572872 | tf_op jit(solution)/shard_map/ppermute | solution.py:36
  4.7 1.4 %collective-permute-start.3 = (bf16[256,1024]{1,0:T(8,128)(2,1)S(1)}, bf16[256,1024]{1,0:T(8,128)(2,1)}, u32[]{:S(2)}, u32[]{:S(2)}) collective-permute-start(bf16[256,1024]{1,0:T(8,128)(2,1)S(1)} %slice_bitcast_fusion.rest_0_), channel_id=1, source_target_pairs={{0,6},{1,7},{2,0},{3,1},{4,2},{5,3},{6,4},{7,5},{8,14},{9,15},{10,... | collective-permute-start | bytes 1572872 | tf_op jit(solution)/shard_map/ppermute | solution.py:36
  6.1 3.7 %collective-permute-start.4 = (bf16[256,1024]{1,0:T(8,128)(2,1)S(1)}, bf16[256,1024]{1,0:T(8,128)(2,1)S(1)}, u32[]{:S(2)}, u32[]{:S(2)}) collective-permute-start(bf16[256,1024]{1,0:T(8,128)(2,1)S(1)} %slice_bitcast_fusion.rest_0_), channel_id=1, source_target_pairs={{0,8},{1,9},{2,10},{3,11},{4,12},{5,13},{6,14},{7,15},{8,0},{9,1},... | collective-permute-start | bytes 1572872 | tf_op jit(solution)/shard_map/ppermute | solution.py:40
  12.5 1.7 %collective-permute-start.8 = (bf16[256,1024]{1,0:T(8,128)(2,1)S(1)}, bf16[256,1024]{1,0:T(8,128)(2,1)}, u32[]{:S(2)}, u32[]{:S(2)}) collective-permute-start(bf16[256,1024]{1,0:T(8,128)(2,1)S(1)} %dequantize.1.own_ref), channel_id=1, source_target_pairs={{0,16},{16,0},{32,48},{48,32},{64,80},{80,64},{96,112},{112,96},{1... | collective-permute-start | bytes 1572872 | tf_op jit(solution)/shard_map/ppermute | solution.py:49
  14.5 2.8 %collective-permute-start.7 = (bf16[256,1024]{1,0:T(8,128)(2,1)S(1)}, bf16[256,1024]{1,0:T(8,128)(2,1)}, u32[]{:S(2)}, u32[]{:S(2)}) collective-permute-start(bf16[256,1024]{1,0:T(8,128)(2,1)S(1)} %slice_bitcast_fusion.rest_0_), channel_id=1, source_target_pairs={{0,4},{1,5},{2,6},{3,7},{4,0},{5,1},{6,2},{7,3},{8,12},{9,13},{10,... | collective-permute-start | bytes 1572872 | tf_op jit(solution)/shard_map/ppermute | solution.py:36
  17.3 7.6 %chip_terms.2 = (bf16[256,1024]{1,0:T(8,128)(2,1)}, bf16[256,1024]{1,0:T(8,128)(2,1)}, bf16[128,1024]{1,0:T(8,128)(2,1)}, bf16[128,1024]{1,0:T(8,128)(2,1)}, bf16[256,1024]{1,0:T(8,128)(2,1)}) custom-call(s32[1]{0:T(128)} %bitcast.order_ref, bf16[768,4096]{1,0:T(8,128)(2,1)} %tok_ref.3, bf16[768,1024]{1,0:T(8,128)(2,1)} %kc_ref.7, ...), custom_call_target="tpu_custom_call" | custom-call | flops 966367616 | bytes 3774873 | tf_op jit(solution)/shard_map/chip_terms/pallas_call | solution.py:121
  25.4 2.4 %collective-permute-start.6 = (bf16[128,1024]{1,0:T(8,128)(2,1)}, bf16[128,1024]{1,0:T(8,128)(2,1)S(1)}, u32[]{:S(2)}, u32[]{:S(2)}) collective-permute-start(bf16[128,1024]{1,0:T(8,128)(2,1)} %get-tuple-element.74), channel_id=1, source_target_pairs={{0,6},{1,7},{2,0},{3,1},{4,2},{5,3},{6,4},{7,5},{8,14},{9,15},{10,... | collective-permute-start | bytes 786440 | tf_op jit(solution)/shard_map/ppermute | solution.py:36
  27.7 3.6 %collective-permute-start.11 = (bf16[256,1024]{1,0:T(8,128)(2,1)}, bf16[256,1024]{1,0:T(8,128)(2,1)S(1)}, u32[]{:S(2)}, u32[]{:S(2)}) collective-permute-start(bf16[256,1024]{1,0:T(8,128)(2,1)} %collective-permute-done.2.rest_2_), channel_id=1, source_target_pairs={{0,8},{1,9},{2,10},{3,11},{4,12},{5,13},{6,14},{7,15},{8,0},{9,1},... | collective-permute-start | bytes 1572872 | tf_op jit(solution)/shard_map/ppermute | solution.py:40
  31.3 7.6 %chip_terms.3 = (bf16[256,1024]{1,0:T(8,128)(2,1)}, bf16[256,1024]{1,0:T(8,128)(2,1)}, bf16[128,1024]{1,0:T(8,128)(2,1)}, bf16[128,1024]{1,0:T(8,128)(2,1)}, bf16[256,1024]{1,0:T(8,128)(2,1)}) custom-call(s32[1]{0:T(128)} %bitcast.order_ref, bf16[768,4096]{1,0:T(8,128)(2,1)} %tok_ref.3, bf16[768,1024]{1,0:T(8,128)(2,1)} %kc_ref.7, ...), custom_call_target="tpu_custom_call" | custom-call | flops 966367616 | bytes 3774873 | tf_op jit(solution)/shard_map/chip_terms/pallas_call | solution.py:121
  42.1 2.7 %collective-permute-start.10 = (bf16[384,1024]{1,0:T(8,128)(2,1)}, bf16[384,1024]{1,0:T(8,128)(2,1)}, u32[]{:S(2)}, u32[]{:S(2)}) collective-permute-start(bf16[384,1024]{1,0:T(8,128)(2,1)} %get-tuple-element.91), channel_id=1, source_target_pairs={{0,6},{1,7},{2,0},{3,1},{4,2},{5,3},{6,4},{7,5},{8,14},{9,15},{10,... | collective-permute-start | bytes 2359304 | tf_op jit(solution)/shard_map/ppermute | solution.py:36
  45.7 1.8 %collective-permute-start.12 = (bf16[256,1024]{1,0:T(8,128)(2,1)}, bf16[256,1024]{1,0:T(8,128)(2,1)}, u32[]{:S(2)}, u32[]{:S(2)}) collective-permute-start(bf16[256,1024]{1,0:T(8,128)(2,1)} %collective-permute-done.3.rest_1_), channel_id=1, source_target_pairs={{0,8},{1,9},{2,10},{3,11},{4,12},{5,13},{6,14},{7,15},{8,0},{9,1},... | collective-permute-start | bytes 1572872 | tf_op jit(solution)/shard_map/ppermute | solution.py:40
  48.6 1.3 %copy-done.3 = bf16[4,256,1024]{2,1,0:T(8,128)(2,1)} copy-done((bf16[4,256,1024]{2,1,0:T(8,128)(2,1)}, bf16[4,256,1024]{2,1,0:T(8,128)(2,1)S(1)}, u32[]{:S(2)}) %copy-start.3) | copy-done | bytes 2097176
  50.0 4.7 %all-to-all-start = ((bf16[4,256,1024]{2,1,0:T(8,128)(2,1)}), bf16[4,256,1024]{2,1,0:T(8,128)(2,1)}, u32[]{:S(2)}, u32[]{:S(2)}) async-start(bf16[4,256,1024]{2,1,0:T(8,128)(2,1)} %copy-done.3), calls=%async_computation | async-start | bytes 4194304 | tf_op jit(solution)/shard_map/all_to_all | solution.py:54
  57.0 6.7 %side_products.2 = (bf16[768,4096]{1,0:T(8,128)(2,1)}, bf16[4,768,256]{2,1,0:T(8,128)(2,1)}) custom-call(s32[1]{0:T(128)} %bitcast.order_ref, bf16[768,1024]{1,0:T(8,128)(2,1)S(1)} %copy-done, bf16[768,1024]{1,0:T(8,128)(2,1)S(1)} %copy-done.2, bf16[256,1024]{1,0:T(8,128)(2,1)S(1)} %copy-done.5, bf16[256,1024]{1,0:T(8,128)(2,1)} %collective-permute-done.3.rest_1_, ...), custom_call_target="tpu_custom_call" | custom-call | flops 966367616 | bytes 2516582 | tf_op jit(solution)/shard_map/side_products/pallas_call | solution.py:174
  63.7 1.8 %relay_home.1 = (bf16[256,1024]{1,0:T(8,128)(2,1)S(1)}, bf16[256,1024]{1,0:T(8,128)(2,1)S(1)}, bf16[256,1024]{1,0:T(8,128)(2,1)S(1)}) custom-call(bf16[256,1024]{1,0:T(8,128)(2,1)S(1)} %copy-done.18, bf16[384,1024]{1,0:T(8,128)(2,1)} %collective-permute-done.9.left_ref, bf16[384,1024]{1,0:T(8,128)(2,1)} %collective-permute-done.10.right_ref, ...), custom_call_target="tpu_custom_call" | custom-call | bytes 1887436 | tf_op jit(solution)/shard_map/relay_home/pallas_call | solution.py:284
  65.6 2.7 %collective-permute-start.16 = (bf16[256,1024]{1,0:T(8,128)(2,1)S(1)}, bf16[256,1024]{1,0:T(8,128)(2,1)S(1)}, u32[]{:S(2)}, u32[]{:S(2)}) collective-permute-start(bf16[256,1024]{1,0:T(8,128)(2,1)S(1)} %get-tuple-element.115), channel_id=1, source_target_pairs={{0,6},{1,7},{2,0},{3,1},{4,2},{5,3},{6,4},{7,5},{8,14},{9,15},{10,... | collective-permute-start | bytes 1572872 | tf_op jit(solution)/shard_map/ppermute | solution.py:36
  68.2 1.8 %collective-permute-start.17 = (bf16[256,1024]{1,0:T(8,128)(2,1)S(1)}, bf16[256,1024]{1,0:T(8,128)(2,1)S(1)}, u32[]{:S(2)}, u32[]{:S(2)}) collective-permute-start(bf16[256,1024]{1,0:T(8,128)(2,1)S(1)} %get-tuple-element.107), channel_id=1, source_target_pairs={{0,8},{1,9},{2,10},{3,11},{4,12},{5,13},{6,14},{7,15},{8,0},{9,1},... | collective-permute-start | bytes 1572872 | tf_op jit(solution)/shard_map/ppermute | solution.py:40
  70.5 2.5 %collective-permute-start.14 = (bf16[4,768,256]{2,1,0:T(8,128)(2,1)}, bf16[4,768,256]{2,1,0:T(8,128)(2,1)}, u32[]{:S(2)}, u32[]{:S(2)}) collective-permute-start(bf16[4,768,256]{2,1,0:T(8,128)(2,1)} %get-tuple-element.100), channel_id=1, source_target_pairs={{0,1},{1,0},{2,3},{3,2},{4,5},{5,4},{6,7},{7,6},{8,9},{9,8},{10,11... | collective-permute-start | bytes 4718600 | tf_op jit(solution)/shard_map/ppermute | solution.py:62
  73.0 6.2 %side_products.3 = (bf16[768,4096]{1,0:T(8,128)(2,1)}, bf16[4,768,256]{2,1,0:T(8,128)(2,1)}) custom-call(s32[1]{0:T(128)} %bitcast.order_ref, bf16[768,1024]{1,0:T(8,128)(2,1)S(1)} %copy-done, bf16[768,1024]{1,0:T(8,128)(2,1)S(1)} %copy-done.2, bf16[256,1024]{1,0:T(8,128)(2,1)S(1)} %copy-done.9, ...), custom_call_target="tpu_custom_call", output_to_operand_aliasing={{0}: (7, {})} | custom-call | flops 966367616 | bytes 2516582 | tf_op jit(solution)/shard_map/side_products/pallas_call | solution.py:174
  81.6 3.3 %collective-permute-start.18 = (bf16[4,768,256]{2,1,0:T(8,128)(2,1)}, bf16[4,768,256]{2,1,0:T(8,128)(2,1)S(1)}, u32[]{:S(2)}, u32[]{:S(2)}) collective-permute-start(bf16[4,768,256]{2,1,0:T(8,128)(2,1)} %get-tuple-element.116), channel_id=1, source_target_pairs={{0,1},{1,0},{2,3},{3,2},{4,5},{5,4},{6,7},{7,6},{8,9},{9,8},{10,11... | collective-permute-start | bytes 4718600 | tf_op jit(solution)/shard_map/ppermute | solution.py:62
  85.7 2.2 %convert_reduce_fusion = f32[256,1024]{1,0:T(8,128)S(1)} fusion(bf16[4,256,1024]{2,1,0:T(8,128)(2,1)} %all-to-all-done), kind=kLoop, calls=%fused_computation | loop fusion | flops 1835008 | bytes 3145728 | tf_op jit(solution)/shard_map/reduce_sum | solution.py:401
  87.9 2.9 %fusion.2 = (bf16[1,256,1024]{2,1,0:T(8,128)(2,1)}, f32[256,1024]{1,0:T(8,128)}, f32[256,1024]{1,0:T(8,128)}) fusion(bf16[1,4,256,1024]{3,2,1,0:T(8,128)(2,1)} %param.10, s32[]{:T(128)S(6)} %select_n.4, f32[256,1024]{1,0:T(8,128)S(1)} %copy-done.25, f32[256,1024]{1,0:T(8,128)S(1)} %convert_reduce_fusion, f32[256,1024]{1,0:T(8,128)S(1)} %copy-done.26), kind=kLoop, calls=%fused_computation.6 | loop fusion | flops 2883584 | bytes 6291460 | tf_op jit(solution)/shard_map/broadcast_in_dim | solution.py:405
  90.8 3.3 %put_blocks.1 = bf16[768,4096]{1,0:T(8,128)(2,1)} custom-call(s32[1]{0:T(128)} %bitcast.order_ref, bf16[4,768,256]{2,1,0:T(8,128)(2,1)} %collective-permute-done.14.rest_0_, bf16[4,768,256]{2,1,0:T(8,128)(2,1)S(1)} %collective-permute-done.18.rest_1_, bf16[768,4096]{1,0:T(8,128)(2,1)} %get-tuple-element.122.rest_2_), custom_call_target="tpu_custom_call", output_to_operand_aliasing={{}: (3, {})} | custom-call | bytes 1887436 | tf_op jit(solution)/shard_map/put_blocks/pallas_call | solution.py:219
  (84 shorter events, 16.1 us)
Async XLA Ops:
  0.6 13.9 %collective-permute-start = (bf16[768,4096]{1,0:T(8,128)(2,1)}, bf16[768,4096]{1,0:T(8,128)(2,1)}, u32[]{:S(2)}, u32[]{:S(2)}) collective-permute-start(bf16[768,4096]{1,0:T(8,128)(2,1)} %tok_ref.3), channel_id=1, source_target_pairs={{0,1},{1,0},{2,3},{3,2},{4,5},{5,4},{6,7},{7,6},{8,9},{9,8},{10,11... | collective-permute-start | bytes 18874376 | tf_op jit(solution)/shard_map/ppermute | solution.py:62
  2.1 10.4 %collective-permute-start.1 = (bf16[768,1024]{1,0:T(8,128)(2,1)}, bf16[768,1024]{1,0:T(8,128)(2,1)S(1)}, u32[]{:S(2)}, u32[]{:S(2)}) collective-permute-start(bf16[768,1024]{1,0:T(8,128)(2,1)} %kc_ref.7), channel_id=1, source_target_pairs={{0,1},{1,0},{2,3},{3,2},{4,5},{5,4},{6,7},{7,6},{8,9},{9,8},{10,11... | collective-permute-start | bytes 4718600 | tf_op jit(solution)/shard_map/ppermute | solution.py:62
  3.3 21.6 %copy-start.4 = (bf16[256,1024]{1,0:T(8,128)(2,1)}, bf16[256,1024]{1,0:T(8,128)(2,1)S(1)}, u32[]{:S(2)}) copy-start(bf16[256,1024]{1,0:T(8,128)(2,1)S(1)} %slice_bitcast_fusion.rest_0_) | copy-start | bytes 1572868
  3.3 21.6 %collective-permute-start.2 = (bf16[256,1024]{1,0:T(8,128)(2,1)S(1)}, bf16[256,1024]{1,0:T(8,128)(2,1)}, u32[]{:S(2)}, u32[]{:S(2)}) collective-permute-start(bf16[256,1024]{1,0:T(8,128)(2,1)S(1)} %slice_bitcast_fusion.rest_0_), channel_id=1, source_target_pairs={{0,2},{1,3},{2,4},{3,5},{4,6},{5,7},{6,0},{7,1},{8,10},{9,11},{10,... | collective-permute-start | bytes 1572872 | tf_op jit(solution)/shard_map/ppermute | solution.py:36
  4.7 20.3 %collective-permute-start.3 = (bf16[256,1024]{1,0:T(8,128)(2,1)S(1)}, bf16[256,1024]{1,0:T(8,128)(2,1)}, u32[]{:S(2)}, u32[]{:S(2)}) collective-permute-start(bf16[256,1024]{1,0:T(8,128)(2,1)S(1)} %slice_bitcast_fusion.rest_0_), channel_id=1, source_target_pairs={{0,6},{1,7},{2,0},{3,1},{4,2},{5,3},{6,4},{7,5},{8,14},{9,15},{10,... | collective-permute-start | bytes 1572872 | tf_op jit(solution)/shard_map/ppermute | solution.py:36
  6.1 18.9 %collective-permute-start.4 = (bf16[256,1024]{1,0:T(8,128)(2,1)S(1)}, bf16[256,1024]{1,0:T(8,128)(2,1)S(1)}, u32[]{:S(2)}, u32[]{:S(2)}) collective-permute-start(bf16[256,1024]{1,0:T(8,128)(2,1)S(1)} %slice_bitcast_fusion.rest_0_), channel_id=1, source_target_pairs={{0,8},{1,9},{2,10},{3,11},{4,12},{5,13},{6,14},{7,15},{8,0},{9,1},... | collective-permute-start | bytes 1572872 | tf_op jit(solution)/shard_map/ppermute | solution.py:40
  12.5 26.4 %collective-permute-start.8 = (bf16[256,1024]{1,0:T(8,128)(2,1)S(1)}, bf16[256,1024]{1,0:T(8,128)(2,1)}, u32[]{:S(2)}, u32[]{:S(2)}) collective-permute-start(bf16[256,1024]{1,0:T(8,128)(2,1)S(1)} %dequantize.1.own_ref), channel_id=1, source_target_pairs={{0,16},{16,0},{32,48},{48,32},{64,80},{80,64},{96,112},{112,96},{1... | collective-permute-start | bytes 1572872 | tf_op jit(solution)/shard_map/ppermute | solution.py:49
  14.5 24.4 %collective-permute-start.7 = (bf16[256,1024]{1,0:T(8,128)(2,1)S(1)}, bf16[256,1024]{1,0:T(8,128)(2,1)}, u32[]{:S(2)}, u32[]{:S(2)}) collective-permute-start(bf16[256,1024]{1,0:T(8,128)(2,1)S(1)} %slice_bitcast_fusion.rest_0_), channel_id=1, source_target_pairs={{0,4},{1,5},{2,6},{3,7},{4,0},{5,1},{6,2},{7,3},{8,12},{9,13},{10,... | collective-permute-start | bytes 1572872 | tf_op jit(solution)/shard_map/ppermute | solution.py:36
  25.0 14.0 %copy-start.8 = (bf16[256,1024]{1,0:T(8,128)(2,1)}, bf16[256,1024]{1,0:T(8,128)(2,1)S(1)}, u32[]{:S(2)}) copy-start(bf16[256,1024]{1,0:T(8,128)(2,1)S(1)} %collective-permute-done.4.rest_0_) | copy-start | bytes 1572868
  25.0 14.0 %copy-start.21 = (bf16[256,1024]{1,0:T(8,128)(2,1)S(1)}, bf16[256,1024]{1,0:T(8,128)(2,1)}, u32[]{:S(2)}) copy-start(bf16[256,1024]{1,0:T(8,128)(2,1)} %get-tuple-element.84.one_ref) | copy-start | bytes 1572868
  25.0 14.0 %copy-start.22 = (bf16[256,1024]{1,0:T(8,128)(2,1)S(1)}, bf16[256,1024]{1,0:T(8,128)(2,1)}, u32[]{:S(2)}) copy-start(bf16[256,1024]{1,0:T(8,128)(2,1)} %get-tuple-element.85.three_ref) | copy-start | bytes 1572868
  25.0 13.9 %collective-permute-start.5 = (bf16[128,1024]{1,0:T(8,128)(2,1)}, bf16[128,1024]{1,0:T(8,128)(2,1)S(1)}, u32[]{:S(2)}, u32[]{:S(2)}) collective-permute-start(bf16[128,1024]{1,0:T(8,128)(2,1)} %get-tuple-element.73), channel_id=1, source_target_pairs={{0,2},{1,3},{2,4},{3,5},{4,6},{5,7},{6,0},{7,1},{8,10},{9,11},{10,... | collective-permute-start | bytes 786440 | tf_op jit(solution)/shard_map/ppermute | solution.py:36
  25.4 13.6 %collective-permute-start.6 = (bf16[128,1024]{1,0:T(8,128)(2,1)}, bf16[128,1024]{1,0:T(8,128)(2,1)S(1)}, u32[]{:S(2)}, u32[]{:S(2)}) collective-permute-start(bf16[128,1024]{1,0:T(8,128)(2,1)} %get-tuple-element.74), channel_id=1, source_target_pairs={{0,6},{1,7},{2,0},{3,1},{4,2},{5,3},{6,4},{7,5},{8,14},{9,15},{10,... | collective-permute-start | bytes 786440 | tf_op jit(solution)/shard_map/ppermute | solution.py:36
  27.7 17.1 %collective-permute-start.11 = (bf16[256,1024]{1,0:T(8,128)(2,1)}, bf16[256,1024]{1,0:T(8,128)(2,1)S(1)}, u32[]{:S(2)}, u32[]{:S(2)}) collective-permute-start(bf16[256,1024]{1,0:T(8,128)(2,1)} %collective-permute-done.2.rest_2_), channel_id=1, source_target_pairs={{0,8},{1,9},{2,10},{3,11},{4,12},{5,13},{6,14},{7,15},{8,0},{9,1},... | collective-permute-start | bytes 1572872 | tf_op jit(solution)/shard_map/ppermute | solution.py:40
  42.1 21.5 %collective-permute-start.9 = (bf16[384,1024]{1,0:T(8,128)(2,1)}, bf16[384,1024]{1,0:T(8,128)(2,1)}, u32[]{:S(2)}, u32[]{:S(2)}) collective-permute-start(bf16[384,1024]{1,0:T(8,128)(2,1)} %get-tuple-element.90), channel_id=1, source_target_pairs={{0,2},{1,3},{2,4},{3,5},{4,6},{5,7},{6,0},{7,1},{8,10},{9,11},{10,... | collective-permute-start | bytes 2359304 | tf_op jit(solution)/shard_map/ppermute | solution.py:36
  42.1 21.5 %collective-permute-start.10 = (bf16[384,1024]{1,0:T(8,128)(2,1)}, bf16[384,1024]{1,0:T(8,128)(2,1)}, u32[]{:S(2)}, u32[]{:S(2)}) collective-permute-start(bf16[384,1024]{1,0:T(8,128)(2,1)} %get-tuple-element.91), channel_id=1, source_target_pairs={{0,6},{1,7},{2,0},{3,1},{4,2},{5,3},{6,4},{7,5},{8,14},{9,15},{10,... | collective-permute-start | bytes 2359304 | tf_op jit(solution)/shard_map/ppermute | solution.py:36
  45.7 18.0 %collective-permute-start.12 = (bf16[256,1024]{1,0:T(8,128)(2,1)}, bf16[256,1024]{1,0:T(8,128)(2,1)}, u32[]{:S(2)}, u32[]{:S(2)}) collective-permute-start(bf16[256,1024]{1,0:T(8,128)(2,1)} %collective-permute-done.3.rest_1_), channel_id=1, source_target_pairs={{0,8},{1,9},{2,10},{3,11},{4,12},{5,13},{6,14},{7,15},{8,0},{9,1},... | collective-permute-start | bytes 1572872 | tf_op jit(solution)/shard_map/ppermute | solution.py:40
  50.0 35.7 %all-to-all-start = ((bf16[4,256,1024]{2,1,0:T(8,128)(2,1)}), bf16[4,256,1024]{2,1,0:T(8,128)(2,1)}, u32[]{:S(2)}, u32[]{:S(2)}) async-start(bf16[4,256,1024]{2,1,0:T(8,128)(2,1)} %copy-done.3), calls=%async_computation | async-start | bytes 4194304 | tf_op jit(solution)/shard_map/all_to_all | solution.py:54
  54.7 15.8 %collective-permute-start.13 = (bf16[256,1024]{1,0:T(8,128)(2,1)}, bf16[256,1024]{1,0:T(8,128)(2,1)S(1)}, u32[]{:S(2)}, u32[]{:S(2)}) collective-permute-start(bf16[256,1024]{1,0:T(8,128)(2,1)} %collective-permute-done.7.rest_3_), channel_id=1, source_target_pairs={{0,8},{1,9},{2,10},{3,11},{4,12},{5,13},{6,14},{7,15},{8,0},{9,1},... | collective-permute-start | bytes 1572872 | tf_op jit(solution)/shard_map/ppermute | solution.py:40
  65.5 13.7 %collective-permute-start.15 = (bf16[256,1024]{1,0:T(8,128)(2,1)S(1)}, bf16[256,1024]{1,0:T(8,128)(2,1)S(1)}, u32[]{:S(2)}, u32[]{:S(2)}) collective-permute-start(bf16[256,1024]{1,0:T(8,128)(2,1)S(1)} %get-tuple-element.114), channel_id=1, source_target_pairs={{0,2},{1,3},{2,4},{3,5},{4,6},{5,7},{6,0},{7,1},{8,10},{9,11},{10,... | collective-permute-start | bytes 1572872 | tf_op jit(solution)/shard_map/ppermute | solution.py:36
  65.6 14.4 %collective-permute-start.16 = (bf16[256,1024]{1,0:T(8,128)(2,1)S(1)}, bf16[256,1024]{1,0:T(8,128)(2,1)S(1)}, u32[]{:S(2)}, u32[]{:S(2)}) collective-permute-start(bf16[256,1024]{1,0:T(8,128)(2,1)S(1)} %get-tuple-element.115), channel_id=1, source_target_pairs={{0,6},{1,7},{2,0},{3,1},{4,2},{5,3},{6,4},{7,5},{8,14},{9,15},{10,... | collective-permute-start | bytes 1572872 | tf_op jit(solution)/shard_map/ppermute | solution.py:36
  68.2 12.6 %collective-permute-start.17 = (bf16[256,1024]{1,0:T(8,128)(2,1)S(1)}, bf16[256,1024]{1,0:T(8,128)(2,1)S(1)}, u32[]{:S(2)}, u32[]{:S(2)}) collective-permute-start(bf16[256,1024]{1,0:T(8,128)(2,1)S(1)} %get-tuple-element.107), channel_id=1, source_target_pairs={{0,8},{1,9},{2,10},{3,11},{4,12},{5,13},{6,14},{7,15},{8,0},{9,1},... | collective-permute-start | bytes 1572872 | tf_op jit(solution)/shard_map/ppermute | solution.py:40
  70.5 20.3 %collective-permute-start.14 = (bf16[4,768,256]{2,1,0:T(8,128)(2,1)}, bf16[4,768,256]{2,1,0:T(8,128)(2,1)}, u32[]{:S(2)}, u32[]{:S(2)}) collective-permute-start(bf16[4,768,256]{2,1,0:T(8,128)(2,1)} %get-tuple-element.100), channel_id=1, source_target_pairs={{0,1},{1,0},{2,3},{3,2},{4,5},{5,4},{6,7},{7,6},{8,9},{9,8},{10,11... | collective-permute-start | bytes 4718600 | tf_op jit(solution)/shard_map/ppermute | solution.py:62
  81.6 9.2 %collective-permute-start.18 = (bf16[4,768,256]{2,1,0:T(8,128)(2,1)}, bf16[4,768,256]{2,1,0:T(8,128)(2,1)S(1)}, u32[]{:S(2)}, u32[]{:S(2)}) collective-permute-start(bf16[4,768,256]{2,1,0:T(8,128)(2,1)} %get-tuple-element.116), channel_id=1, source_target_pairs={{0,1},{1,0},{2,3},{3,2},{4,5},{5,4},{6,7},{7,6},{8,9},{9,8},{10,11... | collective-permute-start | bytes 4718600 | tf_op jit(solution)/shard_map/ppermute | solution.py:62
  (23 other events, 88.5 us)

commit v4 on v3

--- a/solution.py
+++ b/solution.py
@@ -13,7 +13,7 @@
 BLK = 256
 HALF = BLK // 2
 MIB = 1 << 20
-TERM_MIB = 58
+TERM_MIB = 24
 INPUT_MIB = 24
 COST = 0.3
 

time: 95.9 us -> 94.1 us (0.981)
  Pallas kernels: 36.9 us -> 34.3 us
  local copies, waits for them, and re-layouts: 10.7 us -> 12.1 us
    pallas_call x2, Pallas kernels: 15.1 us -> 11.4 us  [chip_terms(): pl.pallas_call(body, grid_spec=pltpu.PrefetchScalarGridSpec(num_scalar_pr...]
    ppermute x4, starting transfers between devices: 7.45 us -> 9.09 us  [to_core(): return lax.ppermute(value, 'fsdp', fsdp_perm(lambda h, x, c: (h, x, 1 - c)))]
    ppermute x5, starting transfers between devices: 12.1 us -> 10.8 us  [to_z(): return lax.ppermute(value, 'fsdp', fsdp_perm(lambda h, x, c: (h + 1, x, c)))]
    ppermute x5, waiting for transfers between devices: 0.47 us -> 1.57 us  [to_z(): return lax.ppermute(value, 'fsdp', fsdp_perm(lambda h, x, c: (h + 1, x, c)))]
    ppermute x1, starting transfers between devices: 1.72 us -> 0.74 us  [to_island(): return lax.ppermute(value, 'island', pairs)]
    unnamed x55 -> x45, local copies, waits for them, and re-layouts: 9.62 us -> 10.2 us
  transfers between devices with their start and end apart: 20 -> 20, of which waited for: 3 -> 2; matrix products, arithmetic and copies ran while one was open for 7% -> 8% of each run, Pallas kernels for 34% -> 32%
where the time goes in v4:
time: 94.1 us; the launch traced here: 93.6 us
  starting transfers between devices  38.8 us (41%)
  Pallas kernels  34.3 us (36%)
  local copies, waits for them, and re-layouts  12.1 us (13%)
  other arithmetic  5.1 us (5%)
  waiting for transfers between devices  1.72 us (2%)
  between operations  1.62 us (2%)
    ppermute x9, starting transfers between devices, to_x(): lax.ppermute(value, 'fsdp', fsdp_perm(lambda h, x, c: (h, x + step, c)))  13.7 us
    pallas_call x2, Pallas kernels, side_products(): pl.pallas_call(body, grid_spec=pltpu.PrefetchScalarGridSpec(num_scalar_pr...  13 us
    pallas_call x2, Pallas kernels, chip_terms(): pl.pallas_call(body, grid_spec=pltpu.PrefetchScalarGridSpec(num_scalar_pr...  11.4 us
    ppermute x5, starting transfers between devices, to_z(): return lax.ppermute(value, 'fsdp', fsdp_perm(lambda h, x, c: (h + 1, x, c)))  10.8 us
    unnamed x45, local copies, waits for them, and re-layouts  10.2 us
    ppermute x4, starting transfers between devices, to_core(): return lax.ppermute(value, 'fsdp', fsdp_perm(lambda h, x, c: (h, x, 1 - c)))  9.09 us
    pallas_call x3, Pallas kernels, plain_kernel(): pl.pallas_call(body, out_shape=[jax.ShapeDtypeStruct(shape, jnp.bfloat16)...  4.5 us
    all_to_all x1, starting transfers between devices, over_y(): lax.all_to_all(copies, 'island', 0, 0, axis_index_groups=groups, tiled=True)  4.45 us
  transfers between devices with their start and end apart: 20, of which 2 were waited for; matrix products, arithmetic and copies ran while one was open for 8% of the time, Pallas kernels for 32%

profile of v4, /device:TPU:1, one launch (start us, length us, event | category | flops | bytes accessed | tf_op | source)
XLA Modules:
  0.0 93.6 jit_solution(5810868312432084228)
XLA Ops:
  0.6 1.5 %collective-permute-start = (bf16[768,4096]{1,0:T(8,128)(2,1)}, bf16[768,4096]{1,0:T(8,128)(2,1)}, u32[]{:S(2)}, u32[]{:S(2)}) collective-permute-start(bf16[768,4096]{1,0:T(8,128)(2,1)} %tok_ref.3), channel_id=1, source_target_pairs={{0,1},{1,0},{2,3},{3,2},{4,5},{5,4},{6,7},{7,6},{8,9},{9,8},{10,11... | collective-permute-start | bytes 18874376 | tf_op jit(solution)/shard_map/ppermute | solution.py:62
  2.2 1.9 %slice_bitcast_fusion.rest_0_ = bf16[256,1024]{1,0:T(8,128)(2,1)} fusion(bf16[1,4,256,1024]{3,2,1,0:T(8,128)(2,1)} %param.10), kind=kLoop, calls=%fused_computation.7 | loop fusion | bytes 1048576 | tf_op jit(solution)/shard_map/squeeze | solution.py:356
  5.4 1.4 %collective-permute-start.3 = (bf16[256,1024]{1,0:T(8,128)(2,1)}, bf16[256,1024]{1,0:T(8,128)(2,1)}, u32[]{:S(2)}, u32[]{:S(2)}) collective-permute-start(bf16[256,1024]{1,0:T(8,128)(2,1)} %slice_bitcast_fusion.rest_0_), channel_id=1, source_target_pairs={{0,6},{1,7},{2,0},{3,1},{4,2},{5,3},{6,4},{7,5},{8,14},{9,15},{10,... | collective-permute-start | bytes 1572872 | tf_op jit(solution)/shard_map/ppermute | solution.py:36
  6.8 3.7 %collective-permute-start.4 = (bf16[256,1024]{1,0:T(8,128)(2,1)}, bf16[256,1024]{1,0:T(8,128)(2,1)}, u32[]{:S(2)}, u32[]{:S(2)}) collective-permute-start(bf16[256,1024]{1,0:T(8,128)(2,1)} %slice_bitcast_fusion.rest_0_), channel_id=1, source_target_pairs={{0,8},{1,9},{2,10},{3,11},{4,12},{5,13},{6,14},{7,15},{8,0},{9,1},... | collective-permute-start | bytes 1572872 | tf_op jit(solution)/shard_map/ppermute | solution.py:40
  14.5 2.8 %collective-permute-start.7 = (bf16[256,1024]{1,0:T(8,128)(2,1)}, bf16[256,1024]{1,0:T(8,128)(2,1)}, u32[]{:S(2)}, u32[]{:S(2)}) collective-permute-start(bf16[256,1024]{1,0:T(8,128)(2,1)} %slice_bitcast_fusion.rest_0_), channel_id=1, source_target_pairs={{0,4},{1,5},{2,6},{3,7},{4,0},{5,1},{6,2},{7,3},{8,12},{9,13},{10,... | collective-permute-start | bytes 1572872 | tf_op jit(solution)/shard_map/ppermute | solution.py:36
  17.4 2.8 %copy-done = bf16[768,4096]{1,0:T(8,128)(2,1)S(1)} copy-done((bf16[768,4096]{1,0:T(8,128)(2,1)S(1)}, bf16[768,4096]{1,0:T(8,128)(2,1)}, u32[]{:S(2)}) %copy-start) | copy-done | bytes 6291480
  20.1 5.7 %chip_terms.2 = (bf16[256,1024]{1,0:T(8,128)(2,1)S(1)}, bf16[256,1024]{1,0:T(8,128)(2,1)S(1)}, bf16[128,1024]{1,0:T(8,128)(2,1)S(1)}, bf16[128,1024]{1,0:T(8,128)(2,1)S(1)}, bf16[256,1024]{1,0:T(8,128)(2,1)S(1)}) custom-call(s32[1]{0:T(128)} %bitcast.order_ref, bf16[768,4096]{1,0:T(8,128)(2,1)S(1)} %copy-done, bf16[768,1024]{1,0:T(8,128)(2,1)S(1)} %copy-done.1, ...), custom_call_target="tpu_custom_call" | custom-call | flops 966367616 | bytes 3774873 | tf_op jit(solution)/shard_map/chip_terms/pallas_call | solution.py:121
  27.0 2.4 %collective-permute-start.6 = (bf16[128,1024]{1,0:T(8,128)(2,1)S(1)}, bf16[128,1024]{1,0:T(8,128)(2,1)S(1)}, u32[]{:S(2)}, u32[]{:S(2)}) collective-permute-start(bf16[128,1024]{1,0:T(8,128)(2,1)S(1)} %get-tuple-element.74), channel_id=1, source_target_pairs={{0,6},{1,7},{2,0},{3,1},{4,2},{5,3},{6,4},{7,5},{8,14},{9,15},{10,... | collective-permute-start | bytes 786440 | tf_op jit(solution)/shard_map/ppermute | solution.py:36
  29.4 3.6 %collective-permute-start.11 = (bf16[256,1024]{1,0:T(8,128)(2,1)}, bf16[256,1024]{1,0:T(8,128)(2,1)S(1)}, u32[]{:S(2)}, u32[]{:S(2)}) collective-permute-start(bf16[256,1024]{1,0:T(8,128)(2,1)} %collective-permute-done.2.rest_2_), channel_id=1, source_target_pairs={{0,8},{1,9},{2,10},{3,11},{4,12},{5,13},{6,14},{7,15},{8,0},{9,1},... | collective-permute-start | bytes 1572872 | tf_op jit(solution)/shard_map/ppermute | solution.py:40
  33.0 5.7 %chip_terms.3 = (bf16[256,1024]{1,0:T(8,128)(2,1)S(1)}, bf16[256,1024]{1,0:T(8,128)(2,1)S(1)}, bf16[128,1024]{1,0:T(8,128)(2,1)S(1)}, bf16[128,1024]{1,0:T(8,128)(2,1)S(1)}, bf16[256,1024]{1,0:T(8,128)(2,1)S(1)}) custom-call(s32[1]{0:T(128)} %bitcast.order_ref, bf16[768,4096]{1,0:T(8,128)(2,1)S(1)} %copy-done, bf16[768,1024]{1,0:T(8,128)(2,1)S(1)} %copy-done.1, ...), custom_call_target="tpu_custom_call" | custom-call | flops 966367616 | bytes 3774873 | tf_op jit(solution)/shard_map/chip_terms/pallas_call | solution.py:121
  38.8 1.4 %relay_away.1 = (bf16[384,1024]{1,0:T(8,128)(2,1)}, bf16[384,1024]{1,0:T(8,128)(2,1)}) custom-call(bf16[256,1024]{1,0:T(8,128)(2,1)S(1)} %get-tuple-element.84.one_ref, bf16[256,1024]{1,0:T(8,128)(2,1)S(1)} %get-tuple-element.85.three_ref, bf16[128,1024]{1,0:T(8,128)(2,1)S(1)} %collective-permute-done.5.left_ref, ...), custom_call_target="tpu_custom_call" | custom-call | bytes 1887436 | tf_op jit(solution)/shard_map/relay_away/pallas_call | solution.py:284
  40.2 2.7 %collective-permute-start.10 = (bf16[384,1024]{1,0:T(8,128)(2,1)}, bf16[384,1024]{1,0:T(8,128)(2,1)}, u32[]{:S(2)}, u32[]{:S(2)}) collective-permute-start(bf16[384,1024]{1,0:T(8,128)(2,1)} %get-tuple-element.91), channel_id=1, source_target_pairs={{0,6},{1,7},{2,0},{3,1},{4,2},{5,3},{6,4},{7,5},{8,14},{9,15},{10,... | collective-permute-start | bytes 2359304 | tf_op jit(solution)/shard_map/ppermute | solution.py:36
  46.9 4.4 %all-to-all-start = ((bf16[4,256,1024]{2,1,0:T(8,128)(2,1)}), bf16[4,256,1024]{2,1,0:T(8,128)(2,1)}, u32[]{:S(2)}, u32[]{:S(2)}) async-start(bf16[4,256,1024]{2,1,0:T(8,128)(2,1)} %copy-done.2), calls=%async_computation | async-start | bytes 4194304 | tf_op jit(solution)/shard_map/all_to_all | solution.py:54
  51.3 2.5 %collective-permute-start.13 = (bf16[256,1024]{1,0:T(8,128)(2,1)}, bf16[256,1024]{1,0:T(8,128)(2,1)S(1)}, u32[]{:S(2)}, u32[]{:S(2)}) collective-permute-start(bf16[256,1024]{1,0:T(8,128)(2,1)} %collective-permute-done.7.rest_3_), channel_id=1, source_target_pairs={{0,8},{1,9},{2,10},{3,11},{4,12},{5,13},{6,14},{7,15},{8,0},{9,1},... | collective-permute-start | bytes 1572872 | tf_op jit(solution)/shard_map/ppermute | solution.py:40
  53.9 6.6 %side_products.2 = (bf16[768,4096]{1,0:T(8,128)(2,1)}, bf16[4,768,256]{2,1,0:T(8,128)(2,1)}) custom-call(s32[1]{0:T(128)} %bitcast.order_ref, bf16[768,1024]{1,0:T(8,128)(2,1)S(1)} %copy-done.1, bf16[768,1024]{1,0:T(8,128)(2,1)S(1)} %collective-permute-done.1.their_kc_ref, bf16[256,1024]{1,0:T(8,128)(2,1)} %slice_bitcast_fusion.rest_0_, ...), custom_call_target="tpu_custom_call" | custom-call | flops 966367616 | bytes 2516582 | tf_op jit(solution)/shard_map/side_products/pallas_call | solution.py:174
  60.6 1.7 %relay_home.1 = (bf16[256,1024]{1,0:T(8,128)(2,1)S(1)}, bf16[256,1024]{1,0:T(8,128)(2,1)S(1)}, bf16[256,1024]{1,0:T(8,128)(2,1)S(1)}) custom-call(bf16[256,1024]{1,0:T(8,128)(2,1)S(1)} %copy-done.15, bf16[384,1024]{1,0:T(8,128)(2,1)} %collective-permute-done.9.left_ref, bf16[384,1024]{1,0:T(8,128)(2,1)} %collective-permute-done.10.right_ref, ...), custom_call_target="tpu_custom_call" | custom-call | bytes 1887436 | tf_op jit(solution)/shard_map/relay_home/pallas_call | solution.py:284
  62.4 2.7 %collective-permute-start.16 = (bf16[256,1024]{1,0:T(8,128)(2,1)S(1)}, bf16[256,1024]{1,0:T(8,128)(2,1)S(1)}, u32[]{:S(2)}, u32[]{:S(2)}) collective-permute-start(bf16[256,1024]{1,0:T(8,128)(2,1)S(1)} %get-tuple-element.115), channel_id=1, source_target_pairs={{0,6},{1,7},{2,0},{3,1},{4,2},{5,3},{6,4},{7,5},{8,14},{9,15},{10,... | collective-permute-start | bytes 1572872 | tf_op jit(solution)/shard_map/ppermute | solution.py:36
  65.6 1.6 %collective-permute-done.13.rest_3_ = bf16[256,1024]{1,0:T(8,128)(2,1)S(1)} collective-permute-done((bf16[256,1024]{1,0:T(8,128)(2,1)}, bf16[256,1024]{1,0:T(8,128)(2,1)S(1)}, u32[]{:S(2)}, u32[]{:S(2)}) %collective-permute-start.13) | collective-permute-done | bytes 524320 | tf_op jit(solution)/shard_map/ppermute | solution.py:40
  67.1 5.8 %collective-permute-start.14 = (bf16[4,768,256]{2,1,0:T(8,128)(2,1)}, bf16[4,768,256]{2,1,0:T(8,128)(2,1)}, u32[]{:S(2)}, u32[]{:S(2)}) collective-permute-start(bf16[4,768,256]{2,1,0:T(8,128)(2,1)} %get-tuple-element.100), channel_id=1, source_target_pairs={{0,1},{1,0},{2,3},{3,2},{4,5},{5,4},{6,7},{7,6},{8,9},{9,8},{10,11... | collective-permute-start | bytes 4718600 | tf_op jit(solution)/shard_map/ppermute | solution.py:62
  73.0 6.3 %side_products.3 = (bf16[768,4096]{1,0:T(8,128)(2,1)}, bf16[4,768,256]{2,1,0:T(8,128)(2,1)}) custom-call(s32[1]{0:T(128)} %bitcast.order_ref, bf16[768,1024]{1,0:T(8,128)(2,1)S(1)} %copy-done.1, bf16[768,1024]{1,0:T(8,128)(2,1)S(1)} %collective-permute-done.1.their_kc_ref, ...), custom_call_target="tpu_custom_call", output_to_operand_aliasing={{0}: (7, {})} | custom-call | flops 966367616 | bytes 2516582 | tf_op jit(solution)/shard_map/side_products/pallas_call | solution.py:174
  81.7 1.7 %collective-permute-start.18 = (bf16[4,768,256]{2,1,0:T(8,128)(2,1)}, bf16[4,768,256]{2,1,0:T(8,128)(2,1)S(1)}, u32[]{:S(2)}, u32[]{:S(2)}) collective-permute-start(bf16[4,768,256]{2,1,0:T(8,128)(2,1)} %get-tuple-element.116), channel_id=1, source_target_pairs={{0,1},{1,0},{2,3},{3,2},{4,5},{5,4},{6,7},{7,6},{8,9},{9,8},{10,11... | collective-permute-start | bytes 4718600 | tf_op jit(solution)/shard_map/ppermute | solution.py:62
  84.1 2.2 %convert_reduce_fusion = f32[256,1024]{1,0:T(8,128)S(1)} fusion(bf16[4,256,1024]{2,1,0:T(8,128)(2,1)} %all-to-all-done), kind=kLoop, calls=%fused_computation | loop fusion | flops 1835008 | bytes 3145728 | tf_op jit(solution)/shard_map/reduce_sum | solution.py:401
  86.3 2.9 %fusion.2 = (bf16[1,256,1024]{2,1,0:T(8,128)(2,1)}, f32[256,1024]{1,0:T(8,128)}, f32[256,1024]{1,0:T(8,128)}) fusion(bf16[1,4,256,1024]{3,2,1,0:T(8,128)(2,1)} %param.10, s32[]{:T(128)S(6)} %select_n.4, f32[256,1024]{1,0:T(8,128)S(1)} %copy-done.20, f32[256,1024]{1,0:T(8,128)S(1)} %convert_reduce_fusion, f32[256,1024]{1,0:T(8,128)S(1)} %copy-done.21), kind=kLoop, calls=%fused_computation.6 | loop fusion | flops 2883584 | bytes 6291460 | tf_op jit(solution)/shard_map/broadcast_in_dim | solution.py:405
  89.2 3.3 %put_blocks.1 = bf16[768,4096]{1,0:T(8,128)(2,1)} custom-call(s32[1]{0:T(128)} %bitcast.order_ref, bf16[4,768,256]{2,1,0:T(8,128)(2,1)} %collective-permute-done.14.rest_0_, bf16[4,768,256]{2,1,0:T(8,128)(2,1)S(1)} %collective-permute-done.18.rest_1_, bf16[768,4096]{1,0:T(8,128)(2,1)} %get-tuple-element.122.rest_2_), custom_call_target="tpu_custom_call", output_to_operand_aliasing={{}: (3, {})} | custom-call | bytes 1887436 | tf_op jit(solution)/shard_map/put_blocks/pallas_call | solution.py:219
  (74 shorter events, 14.7 us)
Async XLA Ops:
  0.6 16.7 %copy-start.1 = (bf16[768,1024]{1,0:T(8,128)(2,1)S(1)}, bf16[768,1024]{1,0:T(8,128)(2,1)}, u32[]{:S(2)}) copy-start(bf16[768,1024]{1,0:T(8,128)(2,1)} %kc_ref.7) | copy-start | bytes 4718596
  0.6 13.9 %collective-permute-start = (bf16[768,4096]{1,0:T(8,128)(2,1)}, bf16[768,4096]{1,0:T(8,128)(2,1)}, u32[]{:S(2)}, u32[]{:S(2)}) collective-permute-start(bf16[768,4096]{1,0:T(8,128)(2,1)} %tok_ref.3), channel_id=1, source_target_pairs={{0,1},{1,0},{2,3},{3,2},{4,5},{5,4},{6,7},{7,6},{8,9},{9,8},{10,11... | collective-permute-start | bytes 18874376 | tf_op jit(solution)/shard_map/ppermute | solution.py:62
  2.1 11.5 %collective-permute-start.1 = (bf16[768,1024]{1,0:T(8,128)(2,1)}, bf16[768,1024]{1,0:T(8,128)(2,1)S(1)}, u32[]{:S(2)}, u32[]{:S(2)}) collective-permute-start(bf16[768,1024]{1,0:T(8,128)(2,1)} %kc_ref.7), channel_id=1, source_target_pairs={{0,1},{1,0},{2,3},{3,2},{4,5},{5,4},{6,7},{7,6},{8,9},{9,8},{10,11... | collective-permute-start | bytes 4718600 | tf_op jit(solution)/shard_map/ppermute | solution.py:62
  4.1 22.5 %collective-permute-start.2 = (bf16[256,1024]{1,0:T(8,128)(2,1)}, bf16[256,1024]{1,0:T(8,128)(2,1)}, u32[]{:S(2)}, u32[]{:S(2)}) collective-permute-start(bf16[256,1024]{1,0:T(8,128)(2,1)} %slice_bitcast_fusion.rest_0_), channel_id=1, source_target_pairs={{0,2},{1,3},{2,4},{3,5},{4,6},{5,7},{6,0},{7,1},{8,10},{9,11},{10,... | collective-permute-start | bytes 1572872 | tf_op jit(solution)/shard_map/ppermute | solution.py:36
  5.4 21.2 %collective-permute-start.3 = (bf16[256,1024]{1,0:T(8,128)(2,1)}, bf16[256,1024]{1,0:T(8,128)(2,1)}, u32[]{:S(2)}, u32[]{:S(2)}) collective-permute-start(bf16[256,1024]{1,0:T(8,128)(2,1)} %slice_bitcast_fusion.rest_0_), channel_id=1, source_target_pairs={{0,6},{1,7},{2,0},{3,1},{4,2},{5,3},{6,4},{7,5},{8,14},{9,15},{10,... | collective-permute-start | bytes 1572872 | tf_op jit(solution)/shard_map/ppermute | solution.py:36
  6.8 19.9 %collective-permute-start.4 = (bf16[256,1024]{1,0:T(8,128)(2,1)}, bf16[256,1024]{1,0:T(8,128)(2,1)}, u32[]{:S(2)}, u32[]{:S(2)}) collective-permute-start(bf16[256,1024]{1,0:T(8,128)(2,1)} %slice_bitcast_fusion.rest_0_), channel_id=1, source_target_pairs={{0,8},{1,9},{2,10},{3,11},{4,12},{5,13},{6,14},{7,15},{8,0},{9,1},... | collective-permute-start | bytes 1572872 | tf_op jit(solution)/shard_map/ppermute | solution.py:40
  13.7 25.0 %collective-permute-start.8 = (bf16[256,1024]{1,0:T(8,128)(2,1)}, bf16[256,1024]{1,0:T(8,128)(2,1)}, u32[]{:S(2)}, u32[]{:S(2)}) collective-permute-start(bf16[256,1024]{1,0:T(8,128)(2,1)} %dequantize.1.own_ref), channel_id=1, source_target_pairs={{0,16},{16,0},{32,48},{48,32},{64,80},{80,64},{96,112},{112,96},{1... | collective-permute-start | bytes 1572872 | tf_op jit(solution)/shard_map/ppermute | solution.py:49
  14.5 24.2 %collective-permute-start.7 = (bf16[256,1024]{1,0:T(8,128)(2,1)}, bf16[256,1024]{1,0:T(8,128)(2,1)}, u32[]{:S(2)}, u32[]{:S(2)}) collective-permute-start(bf16[256,1024]{1,0:T(8,128)(2,1)} %slice_bitcast_fusion.rest_0_), channel_id=1, source_target_pairs={{0,4},{1,5},{2,6},{3,7},{4,0},{5,1},{6,2},{7,3},{8,12},{9,13},{10,... | collective-permute-start | bytes 1572872 | tf_op jit(solution)/shard_map/ppermute | solution.py:36
  26.6 12.1 %collective-permute-start.5 = (bf16[128,1024]{1,0:T(8,128)(2,1)S(1)}, bf16[128,1024]{1,0:T(8,128)(2,1)S(1)}, u32[]{:S(2)}, u32[]{:S(2)}) collective-permute-start(bf16[128,1024]{1,0:T(8,128)(2,1)S(1)} %get-tuple-element.73), channel_id=1, source_target_pairs={{0,2},{1,3},{2,4},{3,5},{4,6},{5,7},{6,0},{7,1},{8,10},{9,11},{10,... | collective-permute-start | bytes 786440 | tf_op jit(solution)/shard_map/ppermute | solution.py:36
  27.0 11.7 %collective-permute-start.6 = (bf16[128,1024]{1,0:T(8,128)(2,1)S(1)}, bf16[128,1024]{1,0:T(8,128)(2,1)S(1)}, u32[]{:S(2)}, u32[]{:S(2)}) collective-permute-start(bf16[128,1024]{1,0:T(8,128)(2,1)S(1)} %get-tuple-element.74), channel_id=1, source_target_pairs={{0,6},{1,7},{2,0},{3,1},{4,2},{5,3},{6,4},{7,5},{8,14},{9,15},{10,... | collective-permute-start | bytes 786440 | tf_op jit(solution)/shard_map/ppermute | solution.py:36
  29.4 13.5 %collective-permute-start.11 = (bf16[256,1024]{1,0:T(8,128)(2,1)}, bf16[256,1024]{1,0:T(8,128)(2,1)S(1)}, u32[]{:S(2)}, u32[]{:S(2)}) collective-permute-start(bf16[256,1024]{1,0:T(8,128)(2,1)} %collective-permute-done.2.rest_2_), channel_id=1, source_target_pairs={{0,8},{1,9},{2,10},{3,11},{4,12},{5,13},{6,14},{7,15},{8,0},{9,1},... | collective-permute-start | bytes 1572872 | tf_op jit(solution)/shard_map/ppermute | solution.py:40
  40.2 20.4 %collective-permute-start.9 = (bf16[384,1024]{1,0:T(8,128)(2,1)}, bf16[384,1024]{1,0:T(8,128)(2,1)}, u32[]{:S(2)}, u32[]{:S(2)}) collective-permute-start(bf16[384,1024]{1,0:T(8,128)(2,1)} %get-tuple-element.90), channel_id=1, source_target_pairs={{0,2},{1,3},{2,4},{3,5},{4,6},{5,7},{6,0},{7,1},{8,10},{9,11},{10,... | collective-permute-start | bytes 2359304 | tf_op jit(solution)/shard_map/ppermute | solution.py:36
  40.2 20.4 %collective-permute-start.10 = (bf16[384,1024]{1,0:T(8,128)(2,1)}, bf16[384,1024]{1,0:T(8,128)(2,1)}, u32[]{:S(2)}, u32[]{:S(2)}) collective-permute-start(bf16[384,1024]{1,0:T(8,128)(2,1)} %get-tuple-element.91), channel_id=1, source_target_pairs={{0,6},{1,7},{2,0},{3,1},{4,2},{5,3},{6,4},{7,5},{8,14},{9,15},{10,... | collective-permute-start | bytes 2359304 | tf_op jit(solution)/shard_map/ppermute | solution.py:36
  43.7 16.9 %collective-permute-start.12 = (bf16[256,1024]{1,0:T(8,128)(2,1)}, bf16[256,1024]{1,0:T(8,128)(2,1)}, u32[]{:S(2)}, u32[]{:S(2)}) collective-permute-start(bf16[256,1024]{1,0:T(8,128)(2,1)} %collective-permute-done.3.rest_1_), channel_id=1, source_target_pairs={{0,8},{1,9},{2,10},{3,11},{4,12},{5,13},{6,14},{7,15},{8,0},{9,1},... | collective-permute-start | bytes 1572872 | tf_op jit(solution)/shard_map/ppermute | solution.py:40
  46.9 37.2 %all-to-all-start = ((bf16[4,256,1024]{2,1,0:T(8,128)(2,1)}), bf16[4,256,1024]{2,1,0:T(8,128)(2,1)}, u32[]{:S(2)}, u32[]{:S(2)}) async-start(bf16[4,256,1024]{2,1,0:T(8,128)(2,1)} %copy-done.2), calls=%async_computation | async-start | bytes 4194304 | tf_op jit(solution)/shard_map/all_to_all | solution.py:54
  51.3 9.2 %copy-start.15 = (bf16[256,1024]{1,0:T(8,128)(2,1)S(1)}, bf16[256,1024]{1,0:T(8,128)(2,1)}, u32[]{:S(2)}) copy-start(bf16[256,1024]{1,0:T(8,128)(2,1)} %copy-done.14) | copy-start | bytes 1572868
  51.3 9.2 %copy-start.17 = (bf16[256,1024]{1,0:T(8,128)(2,1)S(1)}, bf16[256,1024]{1,0:T(8,128)(2,1)}, u32[]{:S(2)}) copy-start(bf16[256,1024]{1,0:T(8,128)(2,1)} %copy-done.16) | copy-start | bytes 1572868
  51.3 15.8 %collective-permute-start.13 = (bf16[256,1024]{1,0:T(8,128)(2,1)}, bf16[256,1024]{1,0:T(8,128)(2,1)S(1)}, u32[]{:S(2)}, u32[]{:S(2)}) collective-permute-start(bf16[256,1024]{1,0:T(8,128)(2,1)} %collective-permute-done.7.rest_3_), channel_id=1, source_target_pairs={{0,8},{1,9},{2,10},{3,11},{4,12},{5,13},{6,14},{7,15},{8,0},{9,1},... | collective-permute-start | bytes 1572872 | tf_op jit(solution)/shard_map/ppermute | solution.py:40
  60.5 12.5 %copy-start.7 = (bf16[256,1024]{1,0:T(8,128)(2,1)S(1)}, bf16[256,1024]{1,0:T(8,128)(2,1)}, u32[]{:S(2)}) copy-start(bf16[256,1024]{1,0:T(8,128)(2,1)} %copy-done.6) | copy-start | bytes 1572868
  62.3 17.0 %collective-permute-start.15 = (bf16[256,1024]{1,0:T(8,128)(2,1)S(1)}, bf16[256,1024]{1,0:T(8,128)(2,1)S(1)}, u32[]{:S(2)}, u32[]{:S(2)}) collective-permute-start(bf16[256,1024]{1,0:T(8,128)(2,1)S(1)} %get-tuple-element.114), channel_id=1, source_target_pairs={{0,2},{1,3},{2,4},{3,5},{4,6},{5,7},{6,0},{7,1},{8,10},{9,11},{10,... | collective-permute-start | bytes 1572872 | tf_op jit(solution)/shard_map/ppermute | solution.py:36
  62.4 17.7 %collective-permute-start.16 = (bf16[256,1024]{1,0:T(8,128)(2,1)S(1)}, bf16[256,1024]{1,0:T(8,128)(2,1)S(1)}, u32[]{:S(2)}, u32[]{:S(2)}) collective-permute-start(bf16[256,1024]{1,0:T(8,128)(2,1)S(1)} %get-tuple-element.115), channel_id=1, source_target_pairs={{0,6},{1,7},{2,0},{3,1},{4,2},{5,3},{6,4},{7,5},{8,14},{9,15},{10,... | collective-permute-start | bytes 1572872 | tf_op jit(solution)/shard_map/ppermute | solution.py:36
  65.1 15.9 %collective-permute-start.17 = (bf16[256,1024]{1,0:T(8,128)(2,1)S(1)}, bf16[256,1024]{1,0:T(8,128)(2,1)S(1)}, u32[]{:S(2)}, u32[]{:S(2)}) collective-permute-start(bf16[256,1024]{1,0:T(8,128)(2,1)S(1)} %get-tuple-element.107), channel_id=1, source_target_pairs={{0,8},{1,9},{2,10},{3,11},{4,12},{5,13},{6,14},{7,15},{8,0},{9,1},... | collective-permute-start | bytes 1572872 | tf_op jit(solution)/shard_map/ppermute | solution.py:40
  67.1 22.1 %collective-permute-start.14 = (bf16[4,768,256]{2,1,0:T(8,128)(2,1)}, bf16[4,768,256]{2,1,0:T(8,128)(2,1)}, u32[]{:S(2)}, u32[]{:S(2)}) collective-permute-start(bf16[4,768,256]{2,1,0:T(8,128)(2,1)} %get-tuple-element.100), channel_id=1, source_target_pairs={{0,1},{1,0},{2,3},{3,2},{4,5},{5,4},{6,7},{7,6},{8,9},{9,8},{10,11... | collective-permute-start | bytes 4718600 | tf_op jit(solution)/shard_map/ppermute | solution.py:62
  81.7 7.5 %collective-permute-start.18 = (bf16[4,768,256]{2,1,0:T(8,128)(2,1)}, bf16[4,768,256]{2,1,0:T(8,128)(2,1)S(1)}, u32[]{:S(2)}, u32[]{:S(2)}) collective-permute-start(bf16[4,768,256]{2,1,0:T(8,128)(2,1)} %get-tuple-element.116), channel_id=1, source_target_pairs={{0,1},{1,0},{2,3},{3,2},{4,5},{5,4},{6,7},{7,6},{8,9},{9,8},{10,11... | collective-permute-start | bytes 4718600 | tf_op jit(solution)/shard_map/ppermute | solution.py:62
  (18 other events, 56.2 us)
